TPU v7x, 128 devices: a whole 4x4x4 slice. The times are simulated.
128 devices in a mesh: row: 8 (over z, core), col: 16 (over x, y).
Axes of the slice: x: 4, y: 4, z: 4, core: 2. Of those that a mesh axis runs over, the one named last changes fastest.
Arguments:
- coords: float32 [16, 65536], replicated, may hold values from -8 to 8
- panel: bfloat16 [65536, 128], P(('row', 'col')), may hold values from -6 to 6
- mixing: float32 [128, 64], replicated, may hold values from -0.5 to 0.5
- owners: int32 [8192, 1], P(('row', 'col')), may hold values from 0 to 127; in each aligned block of 64 rows (0 to 63, 64 to 127, ...) no two rows name the same one
- leaf_picks: int32 [8192, 2], P(('row', 'col')), may hold values from 0 to 1
Outputs:
- bases: bfloat16 [256, 16384], P(('row', 'col'))
- couplings: float32 [8192, 4096], P(('row', 'col'))
Inputs may be any that keep to these rules, and one draw needn't show every extreme that they name: `owners`: among the 64 pairs of one device, no device is named more than 1 times, so the 64 pairs of a device name 64 distinct devices; every device is named somewhere.
All inputs are finite; a program needn't handle non-finite values.
Results may differ from a plain program's by a relative error of at most 0.011.
Values may be sent and summed in bfloat16 or wider, within the bound.
A program may use at most 64 MiB of HBM per device.

v0:
```python
import math

import jax
import jax.numpy as jnp
from jax import lax
from jax.sharding import PartitionSpec as P

LEAF = 256
RANK = 64
NSWEEPS = 6


epsilon = 1e-06


def kernel_tile(left, right):
    highest = lax.Precision.HIGHEST
    left_sq = jnp.sum(left * left, axis=0)
    right_sq = jnp.sum(right * right, axis=0)
    inner_prod = jnp.einsum("dn,dm->nm", left, right, precision=highest)
    squared = left_sq[:, None] + right_sq[None, :] - 2.0 * inner_prod
    return jnp.exp(squared * (-2.0 / left.shape[0])).astype(jnp.bfloat16)


def sketch_rows(row_pts, col_pts, panel_part):
    col_total = col_pts.shape[1]
    step_cols = math.gcd(col_total, 512)

    def add_block(index, total):
        start = index * step_cols
        cols = lax.dynamic_slice_in_dim(col_pts, start, step_cols, 1)
        vectors = lax.dynamic_slice_in_dim(panel_part, start, step_cols, 0)
        return total + jnp.dot(
            kernel_tile(row_pts, cols), vectors, preferred_element_type=jnp.float32
        )

    empty = jnp.zeros((row_pts.shape[1], panel_part.shape[1]), jnp.float32)
    return lax.fori_loop(0, col_total // step_cols, add_block, empty)


def make_bases(leaf_rows, mixing):
    highest = lax.Precision.HIGHEST
    narrow = jnp.einsum("lps,sr->lpr", leaf_rows, mixing, precision=highest)
    gram = jnp.einsum("lpr,lpq->lrq", narrow, narrow, precision=highest)
    scale = jnp.sqrt(jnp.sum(gram * gram, axis=(1, 2)) + epsilon)
    iterate = gram / scale[:, None, None]
    ident = jnp.broadcast_to(jnp.eye(gram.shape[-1], dtype=jnp.float32), gram.shape)
    root = ident
    for sweep in range(NSWEEPS):
        factor = 1.5 * ident - 0.5 * jnp.einsum("lab,lbc->lac", root, iterate, precision=highest)
        iterate = jnp.einsum("lab,lbc->lac", iterate, factor, precision=highest)
        root = jnp.einsum("lab,lbc->lac", factor, root, precision=highest)
    basis = (
        jnp.einsum("lpr,lrq->lpq", narrow, root, precision=highest) / jnp.sqrt(scale)[:, None, None]
    )
    return basis.astype(jnp.bfloat16)


def per_device(coords, panel, mixing, owners, leaf_picks):
    row_count = lax.axis_size("row")
    col_count = lax.axis_size("col")
    row_index = lax.axis_index("row")
    col_index = lax.axis_index("col")
    own_pts = panel.shape[0]
    features = coords.shape[0]
    block_rows = own_pts * col_count
    row_points = lax.dynamic_slice_in_dim(coords, row_index * block_rows, block_rows, 1)
    col_points = lax.dynamic_slice_in_dim(
        coords.reshape(features, row_count, col_count, own_pts), col_index, 1, 2
    )
    col_points = col_points.reshape(features, row_count * own_pts)
    partial_value = sketch_rows(
        row_points, col_points, lax.all_gather(panel, "row", axis=0, tiled=True)
    )
    summed = lax.psum(partial_value, "col")
    mine = lax.dynamic_slice_in_dim(summed, col_index * own_pts, own_pts, 0)
    leaves = own_pts // LEAF
    bases = make_bases(mine.reshape(leaves, LEAF, panel.shape[1]), mixing)
    flat = bases.reshape(leaves, LEAF * RANK)
    owner_ids = owners[:, 0]
    pair_count = owner_ids.shape[0]
    every = lax.all_gather(flat, ("row", "col"), axis=0, tiled=True)
    far = jnp.take(every, owner_ids * leaves + leaf_picks[:, 1], axis=0)
    near = jnp.take(flat, leaf_picks[:, 0], axis=0)
    my_start = (row_index * col_count + col_index) * own_pts
    near_start = my_start + leaf_picks[:, 0] * LEAF
    far_start = (owner_ids * leaves + leaf_picks[:, 1]) * LEAF
    group = math.gcd(pair_count, 16)

    def slice_leaf(offset):
        return lax.dynamic_slice_in_dim(coords, offset, LEAF, 1)

    def couple(items):
        near_rows, far_rows, near_offsets, far_offsets = items
        near_pts = jax.vmap(slice_leaf)(near_offsets)
        far_pts = jax.vmap(slice_leaf)(far_offsets)
        kernels = jax.vmap(kernel_tile)(near_pts, far_pts)
        left = near_rows.reshape(group, LEAF, RANK)
        right = far_rows.reshape(group, LEAF, RANK)
        middle = jnp.einsum(
            "gab,gbr->gar", kernels, right, preferred_element_type=jnp.float32
        ).astype(jnp.bfloat16)
        blocks_out = jnp.einsum("gar,gaq->grq", left, middle, preferred_element_type=jnp.float32)
        return blocks_out.reshape(group, RANK * RANK)

    couplings = lax.map(
        couple,
        (
            near.reshape(-1, group, LEAF * RANK),
            far.reshape(-1, group, LEAF * RANK),
            near_start.reshape(-1, group),
            far_start.reshape(-1, group),
        ),
    )
    return (flat, couplings.reshape(pair_count, RANK * RANK))


def solution(mesh):
    return jax.shard_map(
        per_device,
        mesh=mesh,
        in_specs=(
            P(),
            P(("row", "col"), None),
            P(),
            P(("row", "col"), None),
            P(("row", "col"), None),
        ),
        out_specs=(P(("row", "col"), None), P(("row", "col"), None)),
        check_vma=False,
    )
```

profile of v0, /device:TPU:1, one launch (start us, length us, event | category | flops | bytes accessed | tf_op | source)
XLA Modules:
  0.0 776.9 jit_solution(9915543237015952931)
XLA Ops:
  8.0 6.5 copy.22
  14.5 2.3 dynamic-slice_reduce_fusion
  18.2 18.8 %all-gather.4.cloned.1.call-done = bf16[4096,128]{1,0:T(8,128)(2,1)} async-done(((bf16[512,128]{1,0:T(8,128)(2,1)}), bf16[4096,128]{1,0:T(8,128)(2,1)}) %all-gather.4.cloned.1.call-update) | async-done | bytes 1048592 | tf_op jit(solution)/shard_map/all_gather | solution.py:73
  37.0 218.0 %while.33 = (s32[]{:T(128)}, f32[8192,128]{1,0:T(8,128)}, f32[8192]{0:T(1024)S(1)}, f32[16,4096]{1,0:T(8,128)S(1)}, f32[16,8192]{1,0:T(8,128)S(1)}, /*index=5*/b...) while((s32[]{:T(128)}, f32[8192,128]{1,0:T(8,128)}, f32[8192]{0:T(1024)S(1)}, ...), condition=%wide.region_3.0_spmd.clone, body=%wide.region_1.3_spmd.clone.sunk | while | flops 1902132736 | bytes 25923752 | solution.py:38
  37.0 18.4 %fusion.100 = bf16[8192,512]{0,1:T(8,128)(2,1)} fusion(f32[16,8192]{1,0:T(8,128)S(1)} %get-tuple-element.485, f32[512]{0:T(512)S(1)} %multiply_reduce_fusion.11, f32[8192]{0:T(1024)S(1)} %get-tuple-element.483, f32[16,4096]{1,0:T(8,128)S(1)} %get-tuple-element.484, s32[]{:T(128)S(6)} %select_n.87), kind=kOutput, calls=%fused_computation.23.clone.1 | convolution fusion | flops 826277888 | bytes 8980484 | tf_op jit(solution)/shard_map/while/body/eval_jaxpr/dn,dm->nm/dot_general | solution.py:20
  55.4 7.7 convolution_add_fusion.2
  63.2 18.4 %fusion.100 = bf16[8192,512]{0,1:T(8,128)(2,1)} fusion(f32[16,8192]{1,0:T(8,128)S(1)} %get-tuple-element.485, f32[512]{0:T(512)S(1)} %multiply_reduce_fusion.11, f32[8192]{0:T(1024)S(1)} %get-tuple-element.483, f32[16,4096]{1,0:T(8,128)S(1)} %get-tuple-element.484, s32[]{:T(128)S(6)} %select_n.87), kind=kOutput, calls=%fused_computation.23.clone.1 | convolution fusion | flops 826277888 | bytes 8980484 | tf_op jit(solution)/shard_map/while/body/eval_jaxpr/dn,dm->nm/dot_general | solution.py:20
  81.6 9.0 %convolution_add_fusion.2 = f32[8192,128]{1,0:T(8,128)} fusion(bf16[8192,512]{0,1:T(8,128)(2,1)} %fusion.100, f32[8192,128]{1,0:T(8,128)} %get-tuple-element.472, pred[]{:T(512)S(6)} %compare.9, bf16[4096,128]{1,0:T(8,128)(2,1)} %get-tuple-element.486, s32[]{:T(128)S(6)} %select_n.87), kind=kOutput, calls=%fused_computation.24.clone.1 | convolution fusion | flops 1075838976 | bytes 16908292 | tf_op jit(solution)/shard_map/while/body/eval_jaxpr/dot_general | solution.py:33
  90.6 18.4 %fusion.100 = bf16[8192,512]{0,1:T(8,128)(2,1)} fusion(f32[16,8192]{1,0:T(8,128)S(1)} %get-tuple-element.485, f32[512]{0:T(512)S(1)} %multiply_reduce_fusion.11, f32[8192]{0:T(1024)S(1)} %get-tuple-element.483, f32[16,4096]{1,0:T(8,128)S(1)} %get-tuple-element.484, s32[]{:T(128)S(6)} %select_n.87), kind=kOutput, calls=%fused_computation.23.clone.1 | convolution fusion | flops 826277888 | bytes 8980484 | tf_op jit(solution)/shard_map/while/body/eval_jaxpr/dn,dm->nm/dot_general | solution.py:20
  109.0 9.0 %convolution_add_fusion.2 = f32[8192,128]{1,0:T(8,128)} fusion(bf16[8192,512]{0,1:T(8,128)(2,1)} %fusion.100, f32[8192,128]{1,0:T(8,128)} %get-tuple-element.472, pred[]{:T(512)S(6)} %compare.9, bf16[4096,128]{1,0:T(8,128)(2,1)} %get-tuple-element.486, s32[]{:T(128)S(6)} %select_n.87), kind=kOutput, calls=%fused_computation.24.clone.1 | convolution fusion | flops 1075838976 | bytes 16908292 | tf_op jit(solution)/shard_map/while/body/eval_jaxpr/dot_general | solution.py:33
  118.0 18.4 %fusion.100 = bf16[8192,512]{0,1:T(8,128)(2,1)} fusion(f32[16,8192]{1,0:T(8,128)S(1)} %get-tuple-element.485, f32[512]{0:T(512)S(1)} %multiply_reduce_fusion.11, f32[8192]{0:T(1024)S(1)} %get-tuple-element.483, f32[16,4096]{1,0:T(8,128)S(1)} %get-tuple-element.484, s32[]{:T(128)S(6)} %select_n.87), kind=kOutput, calls=%fused_computation.23.clone.1 | convolution fusion | flops 826277888 | bytes 8980484 | tf_op jit(solution)/shard_map/while/body/eval_jaxpr/dn,dm->nm/dot_general | solution.py:20
  136.4 9.0 %convolution_add_fusion.2 = f32[8192,128]{1,0:T(8,128)} fusion(bf16[8192,512]{0,1:T(8,128)(2,1)} %fusion.100, f32[8192,128]{1,0:T(8,128)} %get-tuple-element.472, pred[]{:T(512)S(6)} %compare.9, bf16[4096,128]{1,0:T(8,128)(2,1)} %get-tuple-element.486, s32[]{:T(128)S(6)} %select_n.87), kind=kOutput, calls=%fused_computation.24.clone.1 | convolution fusion | flops 1075838976 | bytes 16908292 | tf_op jit(solution)/shard_map/while/body/eval_jaxpr/dot_general | solution.py:33
  145.4 18.4 %fusion.100 = bf16[8192,512]{0,1:T(8,128)(2,1)} fusion(f32[16,8192]{1,0:T(8,128)S(1)} %get-tuple-element.485, f32[512]{0:T(512)S(1)} %multiply_reduce_fusion.11, f32[8192]{0:T(1024)S(1)} %get-tuple-element.483, f32[16,4096]{1,0:T(8,128)S(1)} %get-tuple-element.484, s32[]{:T(128)S(6)} %select_n.87), kind=kOutput, calls=%fused_computation.23.clone.1 | convolution fusion | flops 826277888 | bytes 8980484 | tf_op jit(solution)/shard_map/while/body/eval_jaxpr/dn,dm->nm/dot_general | solution.py:20
  163.8 9.0 %convolution_add_fusion.2 = f32[8192,128]{1,0:T(8,128)} fusion(bf16[8192,512]{0,1:T(8,128)(2,1)} %fusion.100, f32[8192,128]{1,0:T(8,128)} %get-tuple-element.472, pred[]{:T(512)S(6)} %compare.9, bf16[4096,128]{1,0:T(8,128)(2,1)} %get-tuple-element.486, s32[]{:T(128)S(6)} %select_n.87), kind=kOutput, calls=%fused_computation.24.clone.1 | convolution fusion | flops 1075838976 | bytes 16908292 | tf_op jit(solution)/shard_map/while/body/eval_jaxpr/dot_general | solution.py:33
  172.8 18.4 %fusion.100 = bf16[8192,512]{0,1:T(8,128)(2,1)} fusion(f32[16,8192]{1,0:T(8,128)S(1)} %get-tuple-element.485, f32[512]{0:T(512)S(1)} %multiply_reduce_fusion.11, f32[8192]{0:T(1024)S(1)} %get-tuple-element.483, f32[16,4096]{1,0:T(8,128)S(1)} %get-tuple-element.484, s32[]{:T(128)S(6)} %select_n.87), kind=kOutput, calls=%fused_computation.23.clone.1 | convolution fusion | flops 826277888 | bytes 8980484 | tf_op jit(solution)/shard_map/while/body/eval_jaxpr/dn,dm->nm/dot_general | solution.py:20
  191.2 9.0 %convolution_add_fusion.2 = f32[8192,128]{1,0:T(8,128)} fusion(bf16[8192,512]{0,1:T(8,128)(2,1)} %fusion.100, f32[8192,128]{1,0:T(8,128)} %get-tuple-element.472, pred[]{:T(512)S(6)} %compare.9, bf16[4096,128]{1,0:T(8,128)(2,1)} %get-tuple-element.486, s32[]{:T(128)S(6)} %select_n.87), kind=kOutput, calls=%fused_computation.24.clone.1 | convolution fusion | flops 1075838976 | bytes 16908292 | tf_op jit(solution)/shard_map/while/body/eval_jaxpr/dot_general | solution.py:33
  200.2 18.4 %fusion.100 = bf16[8192,512]{0,1:T(8,128)(2,1)} fusion(f32[16,8192]{1,0:T(8,128)S(1)} %get-tuple-element.485, f32[512]{0:T(512)S(1)} %multiply_reduce_fusion.11, f32[8192]{0:T(1024)S(1)} %get-tuple-element.483, f32[16,4096]{1,0:T(8,128)S(1)} %get-tuple-element.484, s32[]{:T(128)S(6)} %select_n.87), kind=kOutput, calls=%fused_computation.23.clone.1 | convolution fusion | flops 826277888 | bytes 8980484 | tf_op jit(solution)/shard_map/while/body/eval_jaxpr/dn,dm->nm/dot_general | solution.py:20
  218.6 9.0 %convolution_add_fusion.2 = f32[8192,128]{1,0:T(8,128)} fusion(bf16[8192,512]{0,1:T(8,128)(2,1)} %fusion.100, f32[8192,128]{1,0:T(8,128)} %get-tuple-element.472, pred[]{:T(512)S(6)} %compare.9, bf16[4096,128]{1,0:T(8,128)(2,1)} %get-tuple-element.486, s32[]{:T(128)S(6)} %select_n.87), kind=kOutput, calls=%fused_computation.24.clone.1 | convolution fusion | flops 1075838976 | bytes 16908292 | tf_op jit(solution)/shard_map/while/body/eval_jaxpr/dot_general | solution.py:33
  227.6 18.4 %fusion.100 = bf16[8192,512]{0,1:T(8,128)(2,1)} fusion(f32[16,8192]{1,0:T(8,128)S(1)} %get-tuple-element.485, f32[512]{0:T(512)S(1)} %multiply_reduce_fusion.11, f32[8192]{0:T(1024)S(1)} %get-tuple-element.483, f32[16,4096]{1,0:T(8,128)S(1)} %get-tuple-element.484, s32[]{:T(128)S(6)} %select_n.87), kind=kOutput, calls=%fused_computation.23.clone.1 | convolution fusion | flops 826277888 | bytes 8980484 | tf_op jit(solution)/shard_map/while/body/eval_jaxpr/dn,dm->nm/dot_general | solution.py:20
  246.1 9.0 %convolution_add_fusion.2 = f32[8192,128]{1,0:T(8,128)} fusion(bf16[8192,512]{0,1:T(8,128)(2,1)} %fusion.100, f32[8192,128]{1,0:T(8,128)} %get-tuple-element.472, pred[]{:T(512)S(6)} %compare.9, bf16[4096,128]{1,0:T(8,128)(2,1)} %get-tuple-element.486, s32[]{:T(128)S(6)} %select_n.87), kind=kOutput, calls=%fused_computation.24.clone.1 | convolution fusion | flops 1075838976 | bytes 16908292 | tf_op jit(solution)/shard_map/while/body/eval_jaxpr/dot_general | solution.py:33
  255.3 102.5 %all-reduce.4.cloned.1.call-done = f32[8192,128]{1,0:T(8,128)} async-done(((f32[8192,128]{1,0:T(8,128)}), f32[8192,128]{1,0:T(8,128)}) %all-reduce.4.cloned.1.call-update) | async-done | bytes 4194320 | tf_op jit(solution)/shard_map/psum | solution.py:75
  365.0 1.8 gather_fusion
  366.9 1.6 broadcast_select_fusion.1
  368.5 66.6 %all-gather.6.cloned.1.call-done = bf16[128,2,16384]{2,1,0:T(2,128)(2,1)} async-done(((bf16[1,2,16384]{2,1,0:T(2,128)(2,1)}), bf16[128,2,16384]{2,1,0:T(2,128)(2,1)}) %all-gather.6.cloned.1.call-update) | async-done | bytes 8388624 | tf_op jit(solution)/shard_map/all_gather | solution.py:82
  435.1 13.1 %reshape.192 = bf16[256,16384]{1,0:T(8,128)(2,1)} reshape(bf16[128,2,16384]{2,1,0:T(2,128)(2,1)} %all-gather.6.cloned.1.call-done) | data formatting | bytes 16777216
  448.2 8.1 %gather_fusion.1 = bf16[64,16384]{1,0:T(8,128)(2,1)S(1)} fusion(bf16[256,16384]{1,0:T(8,128)(2,1)} %reshape.192, s32[1024]{0:T(1024)S(1)} %pad_clamp_fusion), kind=kCustom, calls=%fused_computation.1 | custom fusion | bytes 4194560 | tf_op jit(solution)/shard_map/jit(_take)/gather | solution.py:83
  456.3 1.6 broadcast_select_fusion
  458.0 312.4 %while.32 = (s32[]{:T(128)}, f32[4,16,4096]{2,1,0:T(8,128)}, bf16[4,16,16384]{2,1,0:T(8,128)(2,1)}, s32[4,16]{1,0:T(4,128)S(1)}, f32[16,65536]{1,0:T(8,128)}, /*...) while((s32[]{:T(128)}, f32[4,16,4096]{2,1,0:T(8,128)}, ...), condition=%wide.region_9.10_spmd, body=%wide.region_6.9_spmd.sunk | while | flops 374857824 | bytes 12453423 | solution.py:106
  458.0 32.7 %while.34 = (s32[]{:T(128)}, f32[16,65536]{1,0:T(8,128)}, s32[16,2]{0,1:T(2,128)S(1)}, f32[16,16,256]{2,1,0:T(8,128)S(1)}, s32[]{:T(128)}) while((s32[]{:T(128)}, f32[16,65536]{1,0:T(8,128)}, s32[16,2]{0,1:T(2,128)S(1)}, f32[16,16,256]{2,1,0:T(8,128)S(1)}, s32[]{:T(128)}) %tuple.101), condition=%wide.while_cond, body=%wide.while_body.sunk | while | flops 2 | bytes 32865 | solution.py:91
  464.8 1.4 bitcast_dynamic-update-slice_fusion.4
  472.9 1.4 bitcast_dynamic-update-slice_fusion.4
  475.0 1.4 bitcast_dynamic-update-slice_fusion.4
  483.2 1.4 bitcast_dynamic-update-slice_fusion.4
  490.8 32.7 %while.35 = (s32[]{:T(128)}, f32[16,65536]{1,0:T(8,128)}, s32[16,2]{0,1:T(2,128)S(1)}, f32[16,16,256]{2,1,0:T(8,128)S(1)}, s32[]{:T(128)}) while((s32[]{:T(128)}, f32[16,65536]{1,0:T(8,128)}, s32[16,2]{0,1:T(2,128)S(1)}, f32[16,16,256]{2,1,0:T(8,128)S(1)}, s32[]{:T(128)}) %tuple.119), condition=%wide.while_cond.1, body=%wide.while_body.1.sunk | while | flops 2 | bytes 32865 | solution.py:91
  523.6 5.5 exponential_convert_fusion.2
  532.6 2.5 fusion.95
  536.1 32.7 %while.34 = (s32[]{:T(128)}, f32[16,65536]{1,0:T(8,128)}, s32[16,2]{0,1:T(2,128)S(1)}, f32[16,16,256]{2,1,0:T(8,128)S(1)}, s32[]{:T(128)}) while((s32[]{:T(128)}, f32[16,65536]{1,0:T(8,128)}, s32[16,2]{0,1:T(2,128)S(1)}, f32[16,16,256]{2,1,0:T(8,128)S(1)}, s32[]{:T(128)}) %tuple.101), condition=%wide.while_cond, body=%wide.while_body.sunk | while | flops 2 | bytes 32865 | solution.py:91
  568.9 32.7 %while.35 = (s32[]{:T(128)}, f32[16,65536]{1,0:T(8,128)}, s32[16,2]{0,1:T(2,128)S(1)}, f32[16,16,256]{2,1,0:T(8,128)S(1)}, s32[]{:T(128)}) while((s32[]{:T(128)}, f32[16,65536]{1,0:T(8,128)}, s32[16,2]{0,1:T(2,128)S(1)}, f32[16,16,256]{2,1,0:T(8,128)S(1)}, s32[]{:T(128)}) %tuple.119), condition=%wide.while_cond.1, body=%wide.while_body.1.sunk | while | flops 2 | bytes 32865 | solution.py:91
  601.7 5.5 exponential_convert_fusion.2
  610.7 2.5 fusion.95
  614.2 32.7 %while.34 = (s32[]{:T(128)}, f32[16,65536]{1,0:T(8,128)}, s32[16,2]{0,1:T(2,128)S(1)}, f32[16,16,256]{2,1,0:T(8,128)S(1)}, s32[]{:T(128)}) while((s32[]{:T(128)}, f32[16,65536]{1,0:T(8,128)}, s32[16,2]{0,1:T(2,128)S(1)}, f32[16,16,256]{2,1,0:T(8,128)S(1)}, s32[]{:T(128)}) %tuple.101), condition=%wide.while_cond, body=%wide.while_body.sunk | while | flops 2 | bytes 32865 | solution.py:91
  647.0 32.7 %while.35 = (s32[]{:T(128)}, f32[16,65536]{1,0:T(8,128)}, s32[16,2]{0,1:T(2,128)S(1)}, f32[16,16,256]{2,1,0:T(8,128)S(1)}, s32[]{:T(128)}) while((s32[]{:T(128)}, f32[16,65536]{1,0:T(8,128)}, s32[16,2]{0,1:T(2,128)S(1)}, f32[16,16,256]{2,1,0:T(8,128)S(1)}, s32[]{:T(128)}) %tuple.119), condition=%wide.while_cond.1, body=%wide.while_body.1.sunk | while | flops 2 | bytes 32865 | solution.py:91
  679.8 5.5 exponential_convert_fusion.2
  688.8 2.5 fusion.95
  692.3 32.7 %while.34 = (s32[]{:T(128)}, f32[16,65536]{1,0:T(8,128)}, s32[16,2]{0,1:T(2,128)S(1)}, f32[16,16,256]{2,1,0:T(8,128)S(1)}, s32[]{:T(128)}) while((s32[]{:T(128)}, f32[16,65536]{1,0:T(8,128)}, s32[16,2]{0,1:T(2,128)S(1)}, f32[16,16,256]{2,1,0:T(8,128)S(1)}, s32[]{:T(128)}) %tuple.101), condition=%wide.while_cond, body=%wide.while_body.sunk | while | flops 2 | bytes 32865 | solution.py:91
  725.1 32.7 %while.35 = (s32[]{:T(128)}, f32[16,65536]{1,0:T(8,128)}, s32[16,2]{0,1:T(2,128)S(1)}, f32[16,16,256]{2,1,0:T(8,128)S(1)}, s32[]{:T(128)}) while((s32[]{:T(128)}, f32[16,65536]{1,0:T(8,128)}, s32[16,2]{0,1:T(2,128)S(1)}, f32[16,16,256]{2,1,0:T(8,128)S(1)}, s32[]{:T(128)}) %tuple.119), condition=%wide.while_cond.1, body=%wide.while_body.1.sunk | while | flops 2 | bytes 32865 | solution.py:91
  757.8 5.5 exponential_convert_fusion.2
  766.9 2.5 fusion.95
  (489 shorter events, 283.6 us)
Async XLA Ops:
  7.2 351.6 %copy-start = (f32[128,64]{0,1:T(8,128)S(1)}, f32[128,64]{0,1:T(8,128)}, u32[]{:S(2)}) copy-start(f32[128,64]{0,1:T(8,128)} %param.11) | copy-start | bytes 98308
  7.2 29.8 %all-gather.4.cloned.1.call-start = ((), (), s32[]{:S(2)}) async-start(), calls=%async_computation | async-start | bytes 1179648 | tf_op jit(solution)/shard_map/all_gather | solution.py:73
  7.9 349.9 %all-reduce.4.cloned.1.call-start = ((), (), s32[]{:S(2)}) async-start(), calls=%async_computation.1 | async-start | bytes 8388608 | tf_op jit(solution)/shard_map/psum | solution.py:75
  255.0 109.4 %copy-start.2 = (s32[64,2]{0,1:T(2,128)S(1)}, s32[64,2]{0,1:T(2,128)}, u32[]{:S(2)}) copy-start(s32[64,2]{0,1:T(2,128)} %param.13) | copy-start | bytes 1540
  255.0 109.4 %copy-start.3 = (s32[64,1]{0,1:T(1,128)S(1)}, s32[64,1]{0,1:T(1,128)}, u32[]{:S(2)}) copy-start(s32[64,1]{0,1:T(1,128)} %param.12) | copy-start | bytes 772
  255.1 180.0 %all-gather.6.cloned.1.call-start = ((), (), s32[]{:S(2)}) async-start(), calls=%async_computation.2 | async-start | bytes 8454144 | tf_op jit(solution)/shard_map/all_gather | solution.py:82
  365.0 1.9 copy-start.1
Sparse Core Ops, SparseCore 0:
  9.7 27.2 all-gather.3
  255.2 102.5 all-reduce.3
  364.5 70.5 all-gather.5
where the time goes:
time: 787 us; the launch traced here: 777 us
  local copies, waits for them, and re-layouts  314 us (40%)
  matrix products  254 us (32%)
  waiting for transfers between devices  189 us (24%)
  between operations  14 us (2%)
    gather x384, local copies, waits for them, and re-layouts  261 us
    dot_general x12, matrix products, kernel_tile(): inner_prod = jnp.einsum('dn,dm->nm', left, right, precision=highest)  169 us
    psum x1, waiting for transfers between devices, per_device(): summed = lax.psum(partial_value, 'col')  102 us
    dot_general x8, matrix products, add_block(): jnp.dot(kernel_tile(row_pts, cols), vectors, preferred_element_type=jnp.f...  70.5 us
    all_gather x1, waiting for transfers between devices, per_device(): every = lax.all_gather(flat, ('row', 'col'), axis=0, tiled=True)  66.6 us
    unnamed x12, local copies, waits for them, and re-layouts  20.6 us
    all_gather x1, waiting for transfers between devices, per_device(): lax.all_gather(panel, 'row', axis=0, tiled=True)  18.8 us
  transfers between devices with their start and end apart: 3, of which 3 were waited for; matrix products, arithmetic and copies ran while one was open for 2% of the time, Pallas kernels for 0%

commit v1 on v0

v1 whole, which is shorter than its diff:
```python
import functools
import math

import jax
import jax.numpy as jnp
from jax import lax
from jax.experimental import pallas as pl
from jax.experimental.pallas import tpu as pltpu
from jax.sharding import PartitionSpec as P

MESH = pl.DeviceIdType.MESH
HIGHEST = lax.Precision.HIGHEST
f32, bf16 = jnp.float32, jnp.bfloat16

LEAF = 256
RANK = 64
NSWEEPS = 6
EPSILON = 1e-06
OWN = 512
UNIT = 128
UNITS = 4
PAIRS = 64
GROUP = 8
LINES = 32
SIDE = 4
CHUNK = 4096
PART_UNITS = (2, 1, 1)
PART_ROWS = tuple(RANK * u for u in PART_UNITS)
PART_BASE = (0, 128 * SIDE**3, 192 * SIDE**3)
CORE_ROWS = 256 * SIDE**3


def dot(a, b, dims, precision=None):
    return lax.dot_general(
        a, b, (dims, ((), ())), precision=precision, preferred_element_type=f32
    )


def pick3(k, a, b, c):
    return jnp.where(k == 0, a, jnp.where(k == 1, b, c))


def split3(v):
    hi = v.astype(bf16)
    rest = v - hi.astype(f32)
    mid = rest.astype(bf16)
    lo = (rest - mid.astype(f32)).astype(bf16)
    return hi, mid, lo


def features(x, column):
    n = x.shape[1]
    a = x * math.sqrt(4.0 * math.log2(math.e) / x.shape[0])
    h = -0.5 * jnp.sum(a * a, axis=0, keepdims=True)
    hi, mid, lo = split3(a)
    parts = [jnp.broadcast_to(v.astype(f32), (16, n)) for v in split3(h)]
    line = lax.broadcasted_iota(jnp.int32, (16, n), 0)
    at = 0 if column else 3
    extra = jnp.where(line < 6, 1.0, 0.0)
    for k in range(3):
        extra = jnp.where(line == at + k, parts[k], extra)
    extra = extra.astype(bf16)
    zero = jnp.zeros((16, n), bf16)
    if column:
        stack = [hi, hi, mid, mid, hi, lo, extra, zero]
    else:
        stack = [hi, mid, hi, mid, lo, hi, extra, zero]
    return jnp.concatenate(stack, axis=0)


class Place:
    def __init__(self):
        row, col = lax.axis_index("row"), lax.axis_index("col")
        self.core = lax.rem(row, 2)
        self.z = lax.div(row, 2)
        self.x = lax.div(col, SIDE)
        self.y = lax.rem(col, SIDE)
        self.index = row * SIDE * SIDE + col

    def sibling(self):
        return (self.z * 2 + 1 - self.core, self.x * SIDE + self.y)

    def neighbour(self, axis, step):
        x = lax.rem(self.x + jnp.where(axis == 0, step, 0), SIDE)
        y = lax.rem(self.y + jnp.where(axis == 1, step, 0), SIDE)
        z = lax.rem(self.z + jnp.where(axis == 2, step, 0), SIDE)
        return (z * 2 + self.core, x * SIDE + y)

    def along(self, turn):
        c = (self.x, self.y, self.z)
        return [pick3(turn, c[s], c[(s + 1) % 3], c[(s + 2) % 3]) for s in range(3)]


class Gather:
    def __init__(self, place, buf, send, recv, sib_send, sib_recv):
        self.place, self.buf = place, buf
        self.send, self.recv = send, recv
        self.sib_send, self.sib_recv = sib_send, sib_recv

    def turn(self, part):
        return lax.rem(part + self.place.core, 3)

    def start_row(self, part, slot):
        return self.place.core * CORE_ROWS + PART_BASE[part] + slot * PART_ROWS[part]

    def chunk_slot(self, part, stage, v):
        u = self.place.along(self.turn(part))
        if stage == 0:
            return u[2] * 16 + u[1] * 4 + v
        if stage == 1:
            return u[2] * 16 + v * 4
        return v * 16

    def hop(self, part, stage, hop, way):
        turn = self.turn(part)
        v = self.place.along(turn)[stage]
        rows = SIDE**stage * PART_ROWS[part]
        if hop == 0:
            start = self.start_row(part, self.chunk_slot(part, stage, v))
        else:
            from_v = lax.rem(v + (SIDE - 1 if way == 0 else 1), SIDE)
            rows //= 2
            start = self.start_row(part, self.chunk_slot(part, stage, from_v)) + way * rows
        ref = self.buf.at[pl.ds(lax.div(start, LINES), rows // LINES)]
        k = hop * 2 + way
        return pltpu.make_async_remote_copy(
            src_ref=ref,
            dst_ref=ref,
            send_sem=self.send.at[part, stage, k],
            recv_sem=self.recv.at[part, stage, k],
            device_id=self.place.neighbour(lax.rem(turn + stage, 3), 1 if way == 0 else SIDE - 1),
            device_id_type=MESH,
        )

    def side(self, part, piece):
        u2 = self.place.along(self.turn(part))[2]
        plane = lax.rem(u2 + (0, 1, 3, 2)[piece], SIDE)
        start = self.start_row(part, plane * 16)
        ref = self.buf.at[pl.ds(lax.div(start, LINES), 16 * PART_ROWS[part] // LINES)]
        return pltpu.make_async_remote_copy(
            src_ref=ref,
            dst_ref=ref,
            send_sem=self.sib_send.at[part, piece],
            recv_sem=self.sib_recv.at[part, piece],
            device_id=self.place.sibling(),
            device_id_type=MESH,
        )

    def hop_start(self, stage, hop):
        for part in range(3):
            for way in range(2):
                self.hop(part, stage, hop, way).start()

    def hop_wait(self, stage, hop):
        for part in range(3):
            for way in range(2):
                self.hop(part, stage, hop, way).wait_recv()

    def side_start(self, piece):
        for part in range(3):
            self.side(part, piece).start()

    def side_wait(self, piece):
        for part in range(3):
            self.side(part, piece).wait_recv()

    def own_rows(self):
        rows = []
        for part in range(3):
            u = self.place.along(self.turn(part))
            start = self.start_row(part, u[2] * 16 + u[1] * 4 + u[0])
            for unit in range(PART_UNITS[part]):
                rows.append(lax.div(start + unit * RANK, LINES))
        return rows

    def finish_sends(self):
        for part in range(3):
            for stage in range(3):
                for hop in range(2):
                    for way in range(2):
                        self.hop(part, stage, hop, way).wait_send()
            for piece in range(4):
                self.side(part, piece).wait_send()


def inverse_root(gram0, gram1):
    scales = [jnp.sqrt(jnp.sum(g * g) + EPSILON) for g in (gram0, gram1)]
    zero = jnp.zeros((RANK, RANK), f32)
    iterate = jnp.concatenate(
        [
            jnp.concatenate([gram0 / scales[0], zero], axis=1),
            jnp.concatenate([zero, gram1 / scales[1]], axis=1),
        ],
        axis=0,
    )
    shape = (2 * RANK, 2 * RANK)
    ident = jnp.where(
        lax.broadcasted_iota(jnp.int32, shape, 0) == lax.broadcasted_iota(jnp.int32, shape, 1),
        1.0,
        0.0,
    )
    root = ident
    for sweep in range(NSWEEPS):
        product = iterate if sweep == 0 else dot(root, iterate, ((1,), (0,)), HIGHEST)
        factor = 1.5 * ident - 0.5 * product
        if sweep < NSWEEPS - 1:
            iterate = dot(iterate, factor, ((1,), (0,)), HIGHEST)
        root = factor if sweep == 0 else dot(factor, root, ((1,), (0,)), HIGHEST)
    return root, scales


def kernel(
    coords, panel, mixing, rows_of, bases_out, coup_out,
    f_ref, q_ref, b_ref, g_ref, gt_ref, l_ref, bs_ref, sc_ref, sct_ref, st_ref,
    q_send, q_recv, q_sib_send, q_sib_recv, b_send, b_recv, b_sib_send, b_sib_recv,
):
    place = Place()
    gather_q = Gather(place, q_ref, q_send, q_recv, q_sib_send, q_sib_recv)
    gather_b = Gather(place, b_ref, b_send, b_recv, b_sib_send, b_sib_recv)

    barrier = pltpu.get_barrier_semaphore()
    peers = [place.neighbour(axis, step) for axis in range(3) for step in (1, SIDE - 1)]
    peers.append(place.sibling())
    for peer in peers:
        pl.semaphore_signal(barrier, inc=1, device_id=peer, device_id_type=MESH)

    vectors = dot(mixing[...], panel[...].astype(f32), ((0,), (1,)), HIGHEST).astype(bf16)
    for unit, row in enumerate(gather_q.own_rows()):
        for n in range(2):
            q_ref[row + n] = vectors[LINES * n : LINES * (n + 1), unit * UNIT : (unit + 1) * UNIT]
    pl.semaphore_wait(barrier, len(peers))

    gather_q.hop_start(0, 0)
    own = coords[:, pl.ds(pl.multiple_of(place.index * OWN, OWN), OWN)]
    own_features = features(own, False)
    g_ref[...] = own_features
    for leaf in range(2):
        gt_ref[leaf] = own_features[:, leaf * LEAF : (leaf + 1) * LEAF].T
    for stage in range(2):
        gather_q.hop_wait(stage, 0)
        gather_q.hop_start(stage, 1)
        gather_q.hop_wait(stage, 1)
        gather_q.hop_start(stage + 1, 0)
    gather_q.side_start(0)

    def sketch_step(i, total):
        @pl.when(i == 2)
        def _():
            gather_q.side_wait(0)

        @pl.when(i == 4)
        def _():
            gather_q.hop_wait(2, 0)
            gather_q.hop_start(2, 1)
            gather_q.side_start(1)
            gather_q.side_start(2)

        @pl.when(i == 6)
        def _():
            gather_q.side_wait(1)

        @pl.when(i == 10)
        def _():
            gather_q.side_wait(2)

        @pl.when(i == 12)
        def _():
            gather_q.hop_wait(2, 1)
            gather_q.side_start(3)

        @pl.when(i == 14)
        def _():
            gather_q.side_wait(3)

        quarter = lax.div(i, 4)
        step = quarter + jnp.where(quarter == 2, 1, 0) - jnp.where(quarter == 3, 1, 0)
        other = lax.rem(lax.div(i, 2), 2)
        second = lax.rem(i, 2)
        core = lax.rem(place.core + other, 2)
        device_at, row_at = [], []
        for part in range(3):
            turn = lax.rem(part + core, 3)
            w = [pick3(turn, *((4, 1, 32) * 2)[s : s + 3]) for s in range(3)]
            u2 = lax.rem(place.along(turn)[2] + step, SIDE)
            device_at.append((core * 16 + u2 * w[2], w[1], w[0]))
            row_at.append(core * CORE_ROWS + PART_BASE[part] + u2 * 16 * PART_ROWS[part])
        pieces, vectors, places = [], [], []
        for n in range(CHUNK // UNIT):
            slot, unit = n // 2, n % 2
            base, w1, w0 = device_at[0]
            point0 = (base + (slot // 4) * w1 + (slot % 4) * w0) * OWN + unit * UNIT
            row0 = row_at[0] + slot * PART_ROWS[0] + unit * RANK
            slot, part = n % 16, 1 + n // 16
            base, w1, w0 = device_at[part]
            point1 = (base + (slot // 4) * w1 + (slot % 4) * w0) * OWN + (part + 1) * UNIT
            row1 = row_at[part] + slot * PART_ROWS[part]
            point = pl.multiple_of(jnp.where(second == 0, point0, point1), UNIT)
            row = lax.div(jnp.where(second == 0, row0, row1), LINES)
            places.append(point)
            pieces.append(coords[:, pl.ds(point, UNIT)])
            vectors.append(jnp.concatenate([q_ref[row], q_ref[row + 1]], axis=0))
        columns = features(jnp.concatenate(pieces, axis=1), True).T
        for n, point in enumerate(places):
            f_ref[lax.div(point, UNIT)] = columns[n * UNIT : (n + 1) * UNIT, :]
        tile = jnp.exp2(dot(columns, g_ref[...], ((1,), (0,)))).astype(bf16)
        return total + dot(jnp.concatenate(vectors, axis=1), tile, ((1,), (0,)))

    narrow = lax.fori_loop(0, 16, sketch_step, jnp.zeros((RANK, OWN), f32))

    grams = [dot(n, n, ((1,), (1,)), HIGHEST) for n in (narrow[:, :LEAF], narrow[:, LEAF:])]
    root, scales = inverse_root(*grams)
    stacked = jnp.concatenate([narrow[:, :LEAF], narrow[:, LEAF:]], axis=0)
    left = lax.broadcasted_iota(jnp.int32, (1, 2 * RANK), 1) < RANK
    scale = jnp.sqrt(jnp.where(left, scales[0], scales[1]))
    rounded = (dot(stacked, root, ((0,), (0,)), HIGHEST) / scale).astype(bf16)
    for unit, row in enumerate(gather_b.own_rows()):
        for n in range(2):
            at = unit * RANK + LINES * n
            b_ref[row + n] = rounded[at : at + LINES, :]
    gather_b.hop_start(0, 0)

    packed = rounded.astype(f32)
    sc_ref[...] = packed
    flipped = packed.T
    for side in range(2):
        sct_ref[128 * side : 128 * (side + 1), :] = flipped[:, 128 * side : 128 * (side + 1)]
    even, odd = sc_ref[pl.ds(0, 128, stride=2), :], sc_ref[pl.ds(1, 128, stride=2), :]
    bases_out[0] = jnp.where(left, even, pltpu.roll(odd, RANK, 1)).astype(bf16)
    bases_out[1] = jnp.where(left, pltpu.roll(even, RANK, 1), odd).astype(bf16)
    half = RANK // 2
    for leaf in range(2):
        for odd_one in range(2):
            at = odd_one * half
            for side in range(2):
                first = 128 * side + leaf * RANK + odd_one
                bs_ref[leaf, at : at + half, 128 * side : 128 * (side + 1)] = sct_ref[
                    pl.ds(first, half, stride=2), :
                ].astype(bf16)

    def near_step(g, carry):
        for hop in range(4):

            @pl.when(g == hop + 1)
            def _(hop=hop):
                gather_b.hop_wait(hop // 2, hop % 2)
                gather_b.hop_start((hop + 1) // 2, (hop + 1) % 2)
                if hop == 3:
                    gather_b.side_start(0)

        for n in range(GROUP):
            k = g * GROUP + n
            near, far = rows_of[0, k], rows_of[1, k]
            near_rows = gt_ref[near]
            far_rows = jnp.concatenate([f_ref[far], f_ref[far + 1]], axis=0)
            tile = jnp.exp2(dot(near_rows, far_rows, ((1,), (1,)))).astype(bf16)
            l_ref[k] = dot(bs_ref[near], tile, ((1,), (0,))).astype(bf16)
        return carry

    lax.fori_loop(0, PAIRS // GROUP, near_step, 0)

    gather_b.hop_wait(2, 0)
    gather_b.hop_start(2, 1)
    gather_b.side_start(1)
    gather_b.side_start(2)
    gather_b.hop_wait(2, 1)
    gather_b.side_start(3)
    for piece in range(4):
        gather_b.side_wait(piece)

    def far_step(g, carry):
        for pair in range(GROUP):
            k = g * GROUP + pair
            blocks = []
            for part in range(3):
                row = rows_of[2 + part, k]
                for n in range(PART_ROWS[part] // LINES):
                    blocks.append(b_ref[row + n])
            both = dot(
                l_ref[k],
                jnp.concatenate(blocks, axis=0),
                ((1,), (0,)),
            )
            even, odd = both[:half, :], both[half:, :]
            first = jnp.where(left, even, pltpu.roll(odd, RANK, 1))
            second = jnp.where(left, pltpu.roll(even, RANK, 1), odd)
            pick = rows_of[5, k].astype(f32)
            st_ref[pair * half : (pair + 1) * half, :] = first * (1.0 - pick) + second * pick
        rows = pl.ds(pl.multiple_of(g * GROUP, GROUP), GROUP)
        for i in range(half):
            coup_out[rows, 128 * i : 128 * (i + 1)] = st_ref[pl.ds(i, GROUP, stride=half), :]
        return carry

    lax.fori_loop(0, PAIRS // GROUP, far_step, 0)
    gather_q.finish_sends()
    gather_b.finish_sends()


def pair_rows(owner, near, pick):
    line, col = owner // 16, owner % 16
    core, z, x, y = line % 2, line // 2, col // SIDE, col % SIDE
    slots = [z * 16 + y * 4 + x, x * 16 + z * 4 + y, y * 16 + x * 4 + z]
    rows = [near, (owner * 2 + pick) * 2]
    for part in range(3):
        slot = jnp.where(core == 0, slots[part], slots[(part + 1) % 3])
        rows.append((core * CORE_ROWS + PART_BASE[part] + slot * PART_ROWS[part]) // LINES)
    return jnp.stack(rows + [pick])


def per_device(coords, panel, mixing, owners, leaf_picks):
    vmem = pl.BlockSpec(memory_space=pltpu.VMEM)
    smem = pl.BlockSpec(memory_space=pltpu.SMEM)
    sems = pltpu.SemaphoreType.DMA
    points = coords.shape[1]
    bases, couplings = pl.pallas_call(
        kernel,
        out_shape=(
            jax.ShapeDtypeStruct((2, 128, 128), bf16),
            jax.ShapeDtypeStruct((PAIRS, RANK * RANK), f32),
        ),
        in_specs=[vmem, vmem, vmem, smem],
        out_specs=(vmem, vmem),
        scratch_shapes=[
            pltpu.VMEM((points // UNIT, UNIT, 128), bf16),
            pltpu.VMEM((2 * CORE_ROWS // LINES, LINES, 128), bf16),
            pltpu.VMEM((2 * CORE_ROWS // LINES, LINES, 128), bf16),
            pltpu.VMEM((128, OWN), bf16),
            pltpu.VMEM((2, LEAF, 128), bf16),
            pltpu.VMEM((PAIRS, RANK, LEAF), bf16),
            pltpu.VMEM((2, RANK, LEAF), bf16),
            pltpu.VMEM((LEAF, 128), f32),
            pltpu.VMEM((2 * 128, 128), f32),
            pltpu.VMEM((GROUP * RANK // 2, 128), f32),
            sems((3, 3, 4)),
            sems((3, 3, 4)),
            sems((3, 4)),
            sems((3, 4)),
            sems((3, 3, 4)),
            sems((3, 3, 4)),
            sems((3, 4)),
            sems((3, 4)),
        ],
        compiler_params=pltpu.CompilerParams(
            collective_id=0, has_side_effects=True, vmem_limit_bytes=60 * 2**20
        ),
    )(coords, panel, mixing, pair_rows(owners[:, 0], leaf_picks[:, 0], leaf_picks[:, 1]))
    return bases.reshape(2, LEAF * RANK), couplings


def solution(mesh):
    return jax.shard_map(
        per_device,
        mesh=mesh,
        in_specs=(
            P(),
            P(("row", "col"), None),
            P(),
            P(("row", "col"), None),
            P(("row", "col"), None),
        ),
        out_specs=(P(("row", "col"), None), P(("row", "col"), None)),
        check_vma=False,
    )
```

time: 787 us -> 114 us (0.14); the launches traced: 777 us -> 113 us
  local copies, waits for them, and re-layouts: 314 us -> 6.66 us
  matrix products: 254 us -> 0 us
  waiting for transfers between devices: 189 us -> 0 us
  Pallas kernels: 0 us -> 105 us
  between operations: 14 us -> 0.64 us
    gather x386 -> x0, local copies, waits for them, and re-layouts: 271 us -> none
    dot_general x44 -> x0, matrix products: 254 us -> none  [the longest x12 169 us: kernel_tile(): inner_prod = jnp.einsum('dn,dm->nm', left, right, precision=highest)]
    pallas_call x0 -> x1, Pallas kernels: none -> 105 us  [per_device(): pl.pallas_call(kernel, out_shape=(jax.ShapeDtypeStruct((2, 128, 128), bf1...]
    psum x1 -> x0, waiting for transfers between devices: 102 us -> none  [per_device(): summed = lax.psum(partial_value, 'col')]
    all_gather x2 -> x0, waiting for transfers between devices: 85.4 us -> none  [the longest x1 66.6 us: per_device(): every = lax.all_gather(flat, ('row', 'col'), axis=0, tiled=True)]
    unnamed x12 -> x3, local copies, waits for them, and re-layouts: 20.6 us -> 5.29 us
    reshape x9 -> x0, local copies, waits for them, and re-layouts: 9.17 us -> none  [the longest x4 4.51 us: couple(): right = far_rows.reshape(group, LEAF, RANK)]
    dynamic_slice x6 -> x0, local copies, waits for them, and re-layouts: 8.38 us -> none  [the longest x4 5.07 us: per_device(): lax.map(couple, (near.reshape(-1, group, LEAF * RANK), far.reshape(-1, gr...]
  transfers between devices with their start and end apart: 3 -> 0, of which waited for: 3 -> 0; matrix products, arithmetic and copies ran while one was open for 2% -> 0% of each run, Pallas kernels for 0% -> 0%
where the time goes in v1:
time: 114 us; the launch traced here: 113 us
  Pallas kernels  105 us (92%)
  local copies, waits for them, and re-layouts  6.66 us (6%)
    pallas_call x1, Pallas kernels, per_device(): pl.pallas_call(kernel, out_shape=(jax.ShapeDtypeStruct((2, 128, 128), bf1...  105 us
    unnamed x3, local copies, waits for them, and re-layouts  5.29 us

profile of v1, /device:TPU:1, one launch (start us, length us, event | category | flops | bytes accessed | tf_op | source)
XLA Modules:
  0.0 113.4 jit_solution(3553030769234605605)
XLA Ops:
  0.6 0.8 slice_bitcast_fusion
  1.4 0.7 and_select_fusion.8
  2.1 0.6 stack.2.rows_of
  2.8 1.5 %copy.7.mixing = f32[128,64]{1,0:T(8,128)} copy(f32[128,64]{0,1:T(8,128)} %param.7) | data formatting | bytes 65536 | tf_op args[2]
  4.2 105.3 %shard_map.68 = (bf16[2,128,128]{2,1,0:T(8,128)(2,1)}, f32[64,4096]{1,0:T(8,128)}) custom-call(f32[16,65536]{1,0:T(8,128)} %coords.1, bf16[512,128]{1,0:T(8,128)(2,1)} %panel.1, f32[128,64]{1,0:T(8,128)} %copy.7.mixing, s32[6,64]{1,0:T(8,128)} %stack.2.rows_of), custom_call_target="tpu_custom_call" | custom-call | tf_op jit(solution)/shard_map/pallas_call | solution.py:414
  109.6 1.5 %copy.10 = bf16[1,2,128,128]{3,1,2,0:T(2,128)(2,1)} copy(bf16[1,2,128,128]{3,2,1,0:T(8,128)(2,1)} %bitcast.28) | data formatting | bytes 131072
  111.1 2.3 %copy.12 = f32[64,4096]{1,0:T(8,128)} copy(f32[64,4096]{1,0:T(8,128)} %get-tuple-element.21) | data formatting | bytes 2097152
  (2 shorter events, 0.0 us)

commit v2 on v1

--- a/solution.py
+++ b/solution.py
@@ -111,26 +111,32 @@
             return u[2] * 16 + v * 4
         return v * 16
 
-    def hop(self, part, stage, hop, way):
+    def copy(self, part, stage, v, first, count, step, sem):
         turn = self.turn(part)
-        v = self.place.along(turn)[stage]
-        rows = SIDE**stage * PART_ROWS[part]
-        if hop == 0:
-            start = self.start_row(part, self.chunk_slot(part, stage, v))
-        else:
-            from_v = lax.rem(v + (SIDE - 1 if way == 0 else 1), SIDE)
-            rows //= 2
-            start = self.start_row(part, self.chunk_slot(part, stage, from_v)) + way * rows
-        ref = self.buf.at[pl.ds(lax.div(start, LINES), rows // LINES)]
-        k = hop * 2 + way
+        start = self.start_row(part, self.chunk_slot(part, stage, v)) + first
+        ref = self.buf.at[pl.ds(lax.div(start, LINES), count // LINES)]
         return pltpu.make_async_remote_copy(
             src_ref=ref,
             dst_ref=ref,
-            send_sem=self.send.at[part, stage, k],
-            recv_sem=self.recv.at[part, stage, k],
-            device_id=self.place.neighbour(lax.rem(turn + stage, 3), 1 if way == 0 else SIDE - 1),
+            send_sem=self.send.at[part, sem],
+            recv_sem=self.recv.at[part, sem],
+            device_id=self.place.neighbour(lax.rem(turn + stage, 3), step),
             device_id_type=MESH,
         )
+
+    def copies(self, part, what):
+        stage = min(what, 2)
+        v = self.place.along(self.turn(part))[stage]
+        rows = SIDE**stage * PART_ROWS[part]
+        if what < 2:
+            return [self.copy(part, stage, v, 0, rows, s, 3 * what + s - 1) for s in (1, 2, 3)]
+        half = rows // 2
+        result = []
+        for way, step in enumerate((1, SIDE - 1)):
+            first = half * (way if what != 3 else 1 - way)
+            at = v if what < 4 else lax.rem(v + SIDE - step, SIDE)
+            result.append(self.copy(part, stage, at, first, half, step, 2 * what + 2 + way))
+        return result
 
     def side(self, part, piece):
         u2 = self.place.along(self.turn(part))[2]
@@ -146,15 +152,15 @@
             device_id_type=MESH,
         )
 
-    def hop_start(self, stage, hop):
-        for part in range(3):
-            for way in range(2):
-                self.hop(part, stage, hop, way).start()
-
-    def hop_wait(self, stage, hop):
-        for part in range(3):
-            for way in range(2):
-                self.hop(part, stage, hop, way).wait_recv()
+    def start(self, what):
+        for part in range(3):
+            for copy in self.copies(part, what):
+                copy.start()
+
+    def wait(self, what):
+        for part in range(3):
+            for copy in self.copies(part, what):
+                copy.wait_recv()
 
     def side_start(self, piece):
         for part in range(3):
@@ -175,10 +181,9 @@
 
     def finish_sends(self):
         for part in range(3):
-            for stage in range(3):
-                for hop in range(2):
-                    for way in range(2):
-                        self.hop(part, stage, hop, way).wait_send()
+            for what in range(5):
+                for copy in self.copies(part, what):
+                    copy.wait_send()
             for piece in range(4):
                 self.side(part, piece).wait_send()
 
@@ -210,8 +215,8 @@
 
 
 def kernel(
-    coords, panel, mixing, rows_of, bases_out, coup_out,
-    f_ref, q_ref, b_ref, g_ref, gt_ref, l_ref, bs_ref, sc_ref, sct_ref, st_ref,
+    coords, panel, mixing, owners, picks, bases_out, coup_out,
+    x_ref, q_ref, b_ref, k_ref, g_ref, gt_ref, l_ref, bs_ref, sc_ref, sct_ref, st_ref,
     q_send, q_recv, q_sib_send, q_sib_recv, b_send, b_recv, b_sib_send, b_sib_recv,
 ):
     place = Place()
@@ -219,28 +224,47 @@
     gather_b = Gather(place, b_ref, b_send, b_recv, b_sib_send, b_sib_recv)
 
     barrier = pltpu.get_barrier_semaphore()
-    peers = [place.neighbour(axis, step) for axis in range(3) for step in (1, SIDE - 1)]
+    peers = [place.neighbour(axis, step) for axis in range(3) for step in (1, 2, 3)]
     peers.append(place.sibling())
     for peer in peers:
         pl.semaphore_signal(barrier, inc=1, device_id=peer, device_id_type=MESH)
 
-    vectors = dot(mixing[...], panel[...].astype(f32), ((0,), (1,)), HIGHEST).astype(bf16)
+    vectors = dot(mixing[...], panel[...].astype(f32), ((1,), (1,)), HIGHEST).astype(bf16)
     for unit, row in enumerate(gather_q.own_rows()):
         for n in range(2):
             q_ref[row + n] = vectors[LINES * n : LINES * (n + 1), unit * UNIT : (unit + 1) * UNIT]
     pl.semaphore_wait(barrier, len(peers))
 
-    gather_q.hop_start(0, 0)
+    gather_q.start(0)
     own = coords[:, pl.ds(pl.multiple_of(place.index * OWN, OWN), OWN)]
     own_features = features(own, False)
     g_ref[...] = own_features
     for leaf in range(2):
         gt_ref[leaf] = own_features[:, leaf * LEAF : (leaf + 1) * LEAF].T
-    for stage in range(2):
-        gather_q.hop_wait(stage, 0)
-        gather_q.hop_start(stage, 1)
-        gather_q.hop_wait(stage, 1)
-        gather_q.hop_start(stage + 1, 0)
+    for unit in range(coords.shape[1] // UNIT):
+        x_ref[unit] = coords[:, unit * UNIT : (unit + 1) * UNIT]
+
+    def pair_step(g, carry):
+        @pl.when(g == 3)
+        def _():
+            gather_q.wait(0)
+            gather_q.start(1)
+
+        far = []
+        for n in range(GROUP):
+            entry = (owners[0, g * GROUP + n] * 2 + picks[1, g * GROUP + n]) * 2
+            far += [x_ref[entry], x_ref[entry + 1]]
+        far = features(jnp.concatenate(far, axis=1), True)
+        for n in range(GROUP):
+            near_rows = gt_ref[picks[0, g * GROUP + n]]
+            exponent = dot(near_rows, far[:, n * LEAF : (n + 1) * LEAF], ((1,), (0,)))
+            k_ref[g * GROUP + n] = jnp.exp2(exponent).astype(bf16)
+        return carry
+
+    lax.fori_loop(0, PAIRS // GROUP, pair_step, 0)
+    gather_q.wait(1)
+    gather_q.start(2)
+    gather_q.start(3)
     gather_q.side_start(0)
 
     def sketch_step(i, total):
@@ -250,8 +274,9 @@
 
         @pl.when(i == 4)
         def _():
-            gather_q.hop_wait(2, 0)
-            gather_q.hop_start(2, 1)
+            gather_q.wait(2)
+            gather_q.start(4)
+            gather_q.wait(3)
             gather_q.side_start(1)
             gather_q.side_start(2)
 
@@ -265,7 +290,7 @@
 
         @pl.when(i == 12)
         def _():
-            gather_q.hop_wait(2, 1)
+            gather_q.wait(4)
             gather_q.side_start(3)
 
         @pl.when(i == 14)
@@ -284,7 +309,7 @@
             u2 = lax.rem(place.along(turn)[2] + step, SIDE)
             device_at.append((core * 16 + u2 * w[2], w[1], w[0]))
             row_at.append(core * CORE_ROWS + PART_BASE[part] + u2 * 16 * PART_ROWS[part])
-        pieces, vectors, places = [], [], []
+        pieces, vectors = [], []
         for n in range(CHUNK // UNIT):
             slot, unit = n // 2, n % 2
             base, w1, w0 = device_at[0]
@@ -294,14 +319,11 @@
             base, w1, w0 = device_at[part]
             point1 = (base + (slot // 4) * w1 + (slot % 4) * w0) * OWN + (part + 1) * UNIT
             row1 = row_at[part] + slot * PART_ROWS[part]
-            point = pl.multiple_of(jnp.where(second == 0, point0, point1), UNIT)
+            point = jnp.where(second == 0, point0, point1)
             row = lax.div(jnp.where(second == 0, row0, row1), LINES)
-            places.append(point)
-            pieces.append(coords[:, pl.ds(point, UNIT)])
+            pieces.append(x_ref[lax.div(point, UNIT)])
             vectors.append(jnp.concatenate([q_ref[row], q_ref[row + 1]], axis=0))
         columns = features(jnp.concatenate(pieces, axis=1), True).T
-        for n, point in enumerate(places):
-            f_ref[lax.div(point, UNIT)] = columns[n * UNIT : (n + 1) * UNIT, :]
         tile = jnp.exp2(dot(columns, g_ref[...], ((1,), (0,)))).astype(bf16)
         return total + dot(jnp.concatenate(vectors, axis=1), tile, ((1,), (0,)))
 
@@ -317,7 +339,7 @@
         for n in range(2):
             at = unit * RANK + LINES * n
             b_ref[row + n] = rounded[at : at + LINES, :]
-    gather_b.hop_start(0, 0)
+    gather_b.start(0)
 
     packed = rounded.astype(f32)
     sc_ref[...] = packed
@@ -338,31 +360,25 @@
                 ].astype(bf16)
 
     def near_step(g, carry):
-        for hop in range(4):
-
-            @pl.when(g == hop + 1)
-            def _(hop=hop):
-                gather_b.hop_wait(hop // 2, hop % 2)
-                gather_b.hop_start((hop + 1) // 2, (hop + 1) % 2)
-                if hop == 3:
-                    gather_b.side_start(0)
-
         for n in range(GROUP):
             k = g * GROUP + n
-            near, far = rows_of[0, k], rows_of[1, k]
-            near_rows = gt_ref[near]
-            far_rows = jnp.concatenate([f_ref[far], f_ref[far + 1]], axis=0)
-            tile = jnp.exp2(dot(near_rows, far_rows, ((1,), (1,)))).astype(bf16)
-            l_ref[k] = dot(bs_ref[near], tile, ((1,), (0,))).astype(bf16)
+            l_ref[k] = dot(bs_ref[picks[0, k]], k_ref[k], ((1,), (0,))).astype(bf16)
         return carry
 
     lax.fori_loop(0, PAIRS // GROUP, near_step, 0)
 
-    gather_b.hop_wait(2, 0)
-    gather_b.hop_start(2, 1)
+    gather_b.wait(0)
+    gather_b.start(1)
+    gather_b.wait(1)
+    gather_b.start(2)
+    gather_b.start(3)
+    gather_b.side_start(0)
+    gather_b.wait(2)
+    gather_b.start(4)
+    gather_b.wait(3)
     gather_b.side_start(1)
     gather_b.side_start(2)
-    gather_b.hop_wait(2, 1)
+    gather_b.wait(4)
     gather_b.side_start(3)
     for piece in range(4):
         gather_b.side_wait(piece)
@@ -370,9 +386,14 @@
     def far_step(g, carry):
         for pair in range(GROUP):
             k = g * GROUP + pair
+            line, col = lax.div(owners[0, k], 16), lax.rem(owners[0, k], 16)
+            core, z = lax.rem(line, 2), lax.div(line, 2)
+            x, y = lax.div(col, SIDE), lax.rem(col, SIDE)
+            slots = [z * 16 + y * 4 + x, x * 16 + z * 4 + y, y * 16 + x * 4 + z]
             blocks = []
             for part in range(3):
-                row = rows_of[2 + part, k]
+                slot = slots[part] + core * (slots[(part + 1) % 3] - slots[part])
+                row = core * (CORE_ROWS // LINES) + PART_BASE[part] // LINES + slot * (PART_ROWS[part] // LINES)
                 for n in range(PART_ROWS[part] // LINES):
                     blocks.append(b_ref[row + n])
             both = dot(
@@ -383,7 +404,7 @@
             even, odd = both[:half, :], both[half:, :]
             first = jnp.where(left, even, pltpu.roll(odd, RANK, 1))
             second = jnp.where(left, pltpu.roll(even, RANK, 1), odd)
-            pick = rows_of[5, k].astype(f32)
+            pick = picks[1, k].astype(f32)
             st_ref[pair * half : (pair + 1) * half, :] = first * (1.0 - pick) + second * pick
         rows = pl.ds(pl.multiple_of(g * GROUP, GROUP), GROUP)
         for i in range(half):
@@ -393,17 +414,6 @@
     lax.fori_loop(0, PAIRS // GROUP, far_step, 0)
     gather_q.finish_sends()
     gather_b.finish_sends()
-
-
-def pair_rows(owner, near, pick):
-    line, col = owner // 16, owner % 16
-    core, z, x, y = line % 2, line // 2, col // SIDE, col % SIDE
-    slots = [z * 16 + y * 4 + x, x * 16 + z * 4 + y, y * 16 + x * 4 + z]
-    rows = [near, (owner * 2 + pick) * 2]
-    for part in range(3):
-        slot = jnp.where(core == 0, slots[part], slots[(part + 1) % 3])
-        rows.append((core * CORE_ROWS + PART_BASE[part] + slot * PART_ROWS[part]) // LINES)
-    return jnp.stack(rows + [pick])
 
 
 def per_device(coords, panel, mixing, owners, leaf_picks):
@@ -417,12 +427,13 @@
             jax.ShapeDtypeStruct((2, 128, 128), bf16),
             jax.ShapeDtypeStruct((PAIRS, RANK * RANK), f32),
         ),
-        in_specs=[vmem, vmem, vmem, smem],
+        in_specs=[vmem, vmem, vmem, smem, smem],
         out_specs=(vmem, vmem),
         scratch_shapes=[
-            pltpu.VMEM((points // UNIT, UNIT, 128), bf16),
+            pltpu.VMEM((points // UNIT, coords.shape[0], UNIT), f32),
             pltpu.VMEM((2 * CORE_ROWS // LINES, LINES, 128), bf16),
             pltpu.VMEM((2 * CORE_ROWS // LINES, LINES, 128), bf16),
+            pltpu.VMEM((PAIRS, LEAF, LEAF), bf16),
             pltpu.VMEM((128, OWN), bf16),
             pltpu.VMEM((2, LEAF, 128), bf16),
             pltpu.VMEM((PAIRS, RANK, LEAF), bf16),
@@ -430,19 +441,19 @@
             pltpu.VMEM((LEAF, 128), f32),
             pltpu.VMEM((2 * 128, 128), f32),
             pltpu.VMEM((GROUP * RANK // 2, 128), f32),
-            sems((3, 3, 4)),
-            sems((3, 3, 4)),
+            sems((3, 12)),
+            sems((3, 12)),
             sems((3, 4)),
             sems((3, 4)),
-            sems((3, 3, 4)),
-            sems((3, 3, 4)),
+            sems((3, 12)),
+            sems((3, 12)),
             sems((3, 4)),
             sems((3, 4)),
         ],
         compiler_params=pltpu.CompilerParams(
             collective_id=0, has_side_effects=True, vmem_limit_bytes=60 * 2**20
         ),
-    )(coords, panel, mixing, pair_rows(owners[:, 0], leaf_picks[:, 0], leaf_picks[:, 1]))
+    )(coords, panel, mixing.T, owners.T, leaf_picks.T)
     return bases.reshape(2, LEAF * RANK), couplings
 
 

time: 114 us -> 97.8 us (0.86)
  Pallas kernels: 105 us -> 93.2 us
  local copies, waits for them, and re-layouts: 6.66 us -> 3.81 us
    pallas_call x1, Pallas kernels: 105 us -> 93.2 us  [per_device(): pl.pallas_call(kernel, out_shape=(jax.ShapeDtypeStruct((2, 128, 128), bf1...]
    unnamed x3 -> x2, local copies, waits for them, and re-layouts: 5.29 us -> 3.81 us
where the time goes in v2:
time: 97.8 us; the launch traced here: 97.6 us
  Pallas kernels  93.2 us (95%)
  local copies, waits for them, and re-layouts  3.81 us (4%)
    pallas_call x1, Pallas kernels, per_device(): pl.pallas_call(kernel, out_shape=(jax.ShapeDtypeStruct((2, 128, 128), bf1...  93.2 us
    unnamed x2, local copies, waits for them, and re-layouts  3.81 us

profile of v2, /device:TPU:1, one launch (start us, length us, event | category | flops | bytes accessed | tf_op | source)
XLA Modules:
  0.0 97.6 jit_solution(6844261499484864305)
XLA Ops:
  0.6 93.2 %shard_map.68 = (bf16[2,128,128]{2,1,0:T(8,128)(2,1)}, f32[64,4096]{1,0:T(8,128)}) custom-call(f32[16,65536]{1,0:T(8,128)} %coords.1, bf16[512,128]{1,0:T(8,128)(2,1)} %panel.1, f32[64,128]{1,0:T(8,128)} %bitcast.9, s32[1,64]{1,0:T(1,128)} %bitcast.11, s32[2,64]{1,0:T(2,128)} %bitcast.10), custom_call_target="tpu_custom_call" | custom-call | tf_op jit(solution)/shard_map/pallas_call | solution.py:424
  93.8 1.5 %copy.9 = bf16[1,2,128,128]{3,1,2,0:T(2,128)(2,1)} copy(bf16[1,2,128,128]{3,2,1,0:T(8,128)(2,1)} %bitcast.8) | data formatting | bytes 131072
  95.4 2.3 %copy.11 = f32[64,4096]{1,0:T(8,128)} copy(f32[64,4096]{1,0:T(8,128)} %get-tuple-element.9) | data formatting | bytes 2097152

commit v3 on v2

--- a/solution.py
+++ b/solution.py
@@ -24,6 +24,8 @@
 LINES = 32
 SIDE = 4
 CHUNK = 4096
+EARLY = 3
+INPUTS = 8
 PART_UNITS = (2, 1, 1)
 PART_ROWS = tuple(RANK * u for u in PART_UNITS)
 PART_BASE = (0, 128 * SIDE**3, 192 * SIDE**3)
@@ -103,72 +105,109 @@
     def start_row(self, part, slot):
         return self.place.core * CORE_ROWS + PART_BASE[part] + slot * PART_ROWS[part]
 
-    def chunk_slot(self, part, stage, v):
-        u = self.place.along(self.turn(part))
-        if stage == 0:
-            return u[2] * 16 + u[1] * 4 + v
-        if stage == 1:
-            return u[2] * 16 + v * 4
-        return v * 16
-
-    def copy(self, part, stage, v, first, count, step, sem):
-        turn = self.turn(part)
-        start = self.start_row(part, self.chunk_slot(part, stage, v)) + first
-        ref = self.buf.at[pl.ds(lax.div(start, LINES), count // LINES)]
+    def ref(self, part, plane, group, slot, slots):
+        first = lax.rem(plane, SIDE) * 16 + lax.rem(group, SIDE) * 4 + slot
+        start = lax.div(self.start_row(part, first), LINES)
+        return self.buf.at[pl.ds(start, slots * PART_ROWS[part] // LINES)]
+
+    def copy(self, part, stage, ref, step, sem):
         return pltpu.make_async_remote_copy(
             src_ref=ref,
             dst_ref=ref,
             send_sem=self.send.at[part, sem],
             recv_sem=self.recv.at[part, sem],
-            device_id=self.place.neighbour(lax.rem(turn + stage, 3), step),
+            device_id=self.place.neighbour(lax.rem(self.turn(part) + stage, 3), step),
             device_id_type=MESH,
         )
 
-    def copies(self, part, what):
-        stage = min(what, 2)
-        v = self.place.along(self.turn(part))[stage]
-        rows = SIDE**stage * PART_ROWS[part]
-        if what < 2:
-            return [self.copy(part, stage, v, 0, rows, s, 3 * what + s - 1) for s in (1, 2, 3)]
-        half = rows // 2
+    def first(self, stage):
         result = []
-        for way, step in enumerate((1, SIDE - 1)):
-            first = half * (way if what != 3 else 1 - way)
-            at = v if what < 4 else lax.rem(v + SIDE - step, SIDE)
-            result.append(self.copy(part, stage, at, first, half, step, 2 * what + 2 + way))
+        for part in range(3):
+            u = self.place.along(self.turn(part))
+            ref = self.ref(part, u[2], u[1], u[0] if stage == 0 else 0, 1 if stage == 0 else 4)
+            result += [self.copy(part, stage, ref, s, 3 * stage + s - 1) for s in (1, 2, 3)]
         return result
 
-    def side(self, part, piece):
-        u2 = self.place.along(self.turn(part))[2]
-        plane = lax.rem(u2 + (0, 1, 3, 2)[piece], SIDE)
-        start = self.start_row(part, plane * 16)
-        ref = self.buf.at[pl.ds(lax.div(start, LINES), 16 * PART_ROWS[part] // LINES)]
+    def near_plane(self, r):
+        result = []
+        for part in range(3):
+            u = self.place.along(self.turn(part))
+            ref = self.ref(part, u[2], u[1] + r, 0, 4)
+            result += [
+                self.copy(part, 2, ref, s, 6 + 2 * r + way) for way, s in enumerate((1, SIDE - 1))
+            ]
+        return result
+
+    def far_plane(self, r):
+        way = lax.div(r, 2)
+        step = 1 + 2 * way
+        result = []
+        for part in range(3):
+            u = self.place.along(self.turn(part))
+            ref = self.ref(part, u[2] + SIDE - step, u[1] + r, 0, 4)
+            result.append(self.copy(part, 2, ref, step, 14 + r))
+        return result
+
+    def side(self, ref, part, sem):
         return pltpu.make_async_remote_copy(
             src_ref=ref,
             dst_ref=ref,
-            send_sem=self.sib_send.at[part, piece],
-            recv_sem=self.sib_recv.at[part, piece],
+            send_sem=self.sib_send.at[part, sem],
+            recv_sem=self.sib_recv.at[part, sem],
             device_id=self.place.sibling(),
             device_id_type=MESH,
         )
 
-    def start(self, what):
-        for part in range(3):
-            for copy in self.copies(part, what):
-                copy.start()
-
-    def wait(self, what):
-        for part in range(3):
-            for copy in self.copies(part, what):
-                copy.wait_recv()
-
-    def side_start(self, piece):
-        for part in range(3):
-            self.side(part, piece).start()
-
-    def side_wait(self, piece):
-        for part in range(3):
-            self.side(part, piece).wait_recv()
+    def side_own(self):
+        result = []
+        for part in range(3):
+            u = self.place.along(self.turn(part))
+            result.append(self.side(self.ref(part, u[2], 0, 0, 16), part, 0))
+        return result
+
+    def side_near(self, r):
+        result = []
+        for part in range(3):
+            u = self.place.along(self.turn(part))
+            for way, plane in enumerate((3, 1)):
+                ref = self.ref(part, u[2] + plane, u[1] + r, 0, 4)
+                result.append(self.side(ref, part, 1 + 2 * r + way))
+        return result
+
+    def side_far(self, r):
+        result = []
+        for part in range(3):
+            u = self.place.along(self.turn(part))
+            result.append(self.side(self.ref(part, u[2] + 2, u[1] + r, 0, 4), part, 9 + r))
+        return result
+
+    def start(self, copies):
+        for copy in copies:
+            copy.start()
+
+    def wait(self, copies):
+        for copy in copies:
+            copy.wait_recv()
+
+    def second(self):
+        self.wait(self.first(0))
+        self.start(self.first(1))
+        self.start(self.near_plane(0))
+
+    def third(self):
+        self.wait(self.first(1))
+        for r in range(1, 4):
+            self.start(self.near_plane(r))
+        self.start(self.side_own())
+
+    def pass_near(self, r):
+        self.wait(self.near_plane(r))
+        self.start(self.far_plane(r))
+        self.start(self.side_near(r))
+
+    def pass_far(self, r):
+        self.wait(self.far_plane(r))
+        self.start(self.side_far(r))
 
     def own_rows(self):
         rows = []
@@ -180,12 +219,16 @@
         return rows
 
     def finish_sends(self):
-        for part in range(3):
-            for what in range(5):
-                for copy in self.copies(part, what):
-                    copy.wait_send()
-            for piece in range(4):
-                self.side(part, piece).wait_send()
+        for copy in self.first(0) + self.first(1) + self.side_own():
+            copy.wait_send()
+
+        def step(r, carry):
+            copies = self.near_plane(r) + self.far_plane(r) + self.side_near(r) + self.side_far(r)
+            for copy in copies:
+                copy.wait_send()
+            return carry
+
+        lax.fori_loop(0, 4, step, 0)
 
 
 def inverse_root(gram0, gram1):
@@ -216,13 +259,22 @@
 
 def kernel(
     coords, panel, mixing, owners, picks, bases_out, coup_out,
-    x_ref, q_ref, b_ref, k_ref, g_ref, gt_ref, l_ref, bs_ref, sc_ref, sct_ref, st_ref,
-    q_send, q_recv, q_sib_send, q_sib_recv, b_send, b_recv, b_sib_send, b_sib_recv,
+    in_ref, x_ref, pre_ref, q_ref, b_ref, k_ref, g_ref, gt_ref, l_ref, bs_ref, sc_ref, sct_ref, st_ref,
+    in_sem, q_send, q_recv, q_sib_send, q_sib_recv, b_send, b_recv, b_sib_send, b_sib_recv,
 ):
     place = Place()
     gather_q = Gather(place, q_ref, q_send, q_recv, q_sib_send, q_sib_recv)
     gather_b = Gather(place, b_ref, b_send, b_recv, b_sib_send, b_sib_recv)
 
+    width = coords.shape[1] // INPUTS
+
+    def load(j):
+        return pltpu.make_async_copy(
+            coords.at[:, j * width : (j + 1) * width], in_ref.at[j % 2], in_sem.at[j % 2]
+        )
+
+    load(0).start()
+    load(1).start()
     barrier = pltpu.get_barrier_semaphore()
     peers = [place.neighbour(axis, step) for axis in range(3) for step in (1, 2, 3)]
     peers.append(place.sibling())
@@ -235,20 +287,23 @@
             q_ref[row + n] = vectors[LINES * n : LINES * (n + 1), unit * UNIT : (unit + 1) * UNIT]
     pl.semaphore_wait(barrier, len(peers))
 
-    gather_q.start(0)
-    own = coords[:, pl.ds(pl.multiple_of(place.index * OWN, OWN), OWN)]
-    own_features = features(own, False)
+    gather_q.start(gather_q.first(0))
+    for j in range(INPUTS):
+        load(j).wait()
+        for unit in range(width // UNIT):
+            x_ref[j * width // UNIT + unit] = in_ref[j % 2, :, unit * UNIT : (unit + 1) * UNIT]
+        if j + 2 < INPUTS:
+            load(j + 2).start()
+    own = [x_ref[place.index * UNITS + unit] for unit in range(UNITS)]
+    own_features = features(jnp.concatenate(own, axis=1), False)
     g_ref[...] = own_features
     for leaf in range(2):
         gt_ref[leaf] = own_features[:, leaf * LEAF : (leaf + 1) * LEAF].T
-    for unit in range(coords.shape[1] // UNIT):
-        x_ref[unit] = coords[:, unit * UNIT : (unit + 1) * UNIT]
 
     def pair_step(g, carry):
-        @pl.when(g == 3)
+        @pl.when(g == 6)
         def _():
-            gather_q.wait(0)
-            gather_q.start(1)
+            gather_q.second()
 
         far = []
         for n in range(GROUP):
@@ -262,72 +317,82 @@
         return carry
 
     lax.fori_loop(0, PAIRS // GROUP, pair_step, 0)
-    gather_q.wait(1)
-    gather_q.start(2)
-    gather_q.start(3)
-    gather_q.side_start(0)
-
-    def sketch_step(i, total):
+
+    def chunk(i):
+        in_own, in_far = i < 4, i >= 12
+        other = jnp.where(in_own, lax.div(i, 2), lax.rem(i, 2))
+        core = lax.rem(place.core + other, 2)
+        r = jnp.where(in_far, lax.div(i + 4, 2) - 8, jnp.where(in_own, 2 * lax.rem(i, 2), lax.div(i, 2) - 2))
+        groups = (r, r + jnp.where(in_far, 2, jnp.where(in_own, 1, 0)))
+        planes = [jnp.where(in_far, 2, jnp.where(in_own, 0, p)) for p in (3, 1)]
+        units = []
+        for half in range(2):
+            for unit in range(UNITS):
+                part = max(unit - 1, 0)
+                turn = lax.rem(part + core, 3)
+                w = [pick3(turn, *((4, 1, 32) * 2)[s : s + 3]) for s in range(3)]
+                u = place.along(turn)
+                u2, u1 = lax.rem(u[2] + planes[half], SIDE), lax.rem(u[1] + groups[half], SIDE)
+                device = core * 16 + u2 * w[2] + u1 * w[1]
+                entry = core * (CORE_ROWS // LINES) + PART_BASE[part] // LINES
+                size = PART_ROWS[part] // LINES
+                entry = entry + (u2 * 16 + u1 * 4) * size + (unit % 2 if part == 0 else 0) * 2
+                for u0 in range(SIDE):
+                    units.append(((device + u0 * w[0]) * UNITS + unit, entry + u0 * size))
+        return units
+
+    def chunk_tile(i):
+        columns = features(jnp.concatenate([x_ref[p] for p, _ in chunk(i)], axis=1), True).T
+        return jnp.exp2(dot(columns, g_ref[...], ((1,), (0,)))).astype(bf16)
+
+    def chunk_vectors(i):
+        vectors = [jnp.concatenate([q_ref[v], q_ref[v + 1]], axis=0) for _, v in chunk(i)]
+        return jnp.concatenate(vectors, axis=1)
+
+    def early_tile(i, carry):
+        pre_ref[i] = chunk_tile(i)
+        return carry
+
+    lax.fori_loop(0, EARLY, early_tile, 0)
+    gather_q.third()
+
+    def await_side(i):
         @pl.when(i == 2)
         def _():
-            gather_q.side_wait(0)
-
-        @pl.when(i == 4)
+            gather_q.wait(gather_q.side_own())
+
+    def early_step(i, total):
+        await_side(i)
+        return total + dot(chunk_vectors(i), pre_ref[i], ((1,), (0,)))
+
+    total = lax.fori_loop(0, EARLY, early_step, jnp.zeros((RANK, OWN), f32))
+
+    def sketch_step(i, total):
+        await_side(i)
+        even = lax.rem(i, 2) == 0
+
+        @pl.when((i >= 4) & (i < 12) & even)
         def _():
-            gather_q.wait(2)
-            gather_q.start(4)
-            gather_q.wait(3)
-            gather_q.side_start(1)
-            gather_q.side_start(2)
-
-        @pl.when(i == 6)
+            gather_q.pass_near(lax.div(i, 2) - 2)
+
+        @pl.when((i >= 4) & (i < 12) & jnp.logical_not(even))
         def _():
-            gather_q.side_wait(1)
-
-        @pl.when(i == 10)
+            gather_q.wait(gather_q.side_near(lax.div(i, 2) - 2))
+
+        @pl.when((i >= 12) & even)
         def _():
-            gather_q.side_wait(2)
-
-        @pl.when(i == 12)
+            gather_q.pass_far(lax.div(i, 2) - 6)
+            gather_q.pass_far(lax.div(i, 2) - 4)
+
+        @pl.when((i >= 12) & jnp.logical_not(even))
         def _():
-            gather_q.wait(4)
-            gather_q.side_start(3)
-
-        @pl.when(i == 14)
-        def _():
-            gather_q.side_wait(3)
-
-        quarter = lax.div(i, 4)
-        step = quarter + jnp.where(quarter == 2, 1, 0) - jnp.where(quarter == 3, 1, 0)
-        other = lax.rem(lax.div(i, 2), 2)
-        second = lax.rem(i, 2)
-        core = lax.rem(place.core + other, 2)
-        device_at, row_at = [], []
-        for part in range(3):
-            turn = lax.rem(part + core, 3)
-            w = [pick3(turn, *((4, 1, 32) * 2)[s : s + 3]) for s in range(3)]
-            u2 = lax.rem(place.along(turn)[2] + step, SIDE)
-            device_at.append((core * 16 + u2 * w[2], w[1], w[0]))
-            row_at.append(core * CORE_ROWS + PART_BASE[part] + u2 * 16 * PART_ROWS[part])
-        pieces, vectors = [], []
-        for n in range(CHUNK // UNIT):
-            slot, unit = n // 2, n % 2
-            base, w1, w0 = device_at[0]
-            point0 = (base + (slot // 4) * w1 + (slot % 4) * w0) * OWN + unit * UNIT
-            row0 = row_at[0] + slot * PART_ROWS[0] + unit * RANK
-            slot, part = n % 16, 1 + n // 16
-            base, w1, w0 = device_at[part]
-            point1 = (base + (slot // 4) * w1 + (slot % 4) * w0) * OWN + (part + 1) * UNIT
-            row1 = row_at[part] + slot * PART_ROWS[part]
-            point = jnp.where(second == 0, point0, point1)
-            row = lax.div(jnp.where(second == 0, row0, row1), LINES)
-            pieces.append(x_ref[lax.div(point, UNIT)])
-            vectors.append(jnp.concatenate([q_ref[row], q_ref[row + 1]], axis=0))
-        columns = features(jnp.concatenate(pieces, axis=1), True).T
-        tile = jnp.exp2(dot(columns, g_ref[...], ((1,), (0,)))).astype(bf16)
-        return total + dot(jnp.concatenate(vectors, axis=1), tile, ((1,), (0,)))
-
-    narrow = lax.fori_loop(0, 16, sketch_step, jnp.zeros((RANK, OWN), f32))
+            gather_q.wait(gather_q.side_far(lax.div(i, 2) - 6))
+            gather_q.wait(gather_q.side_far(lax.div(i, 2) - 4))
+
+        tile = chunk_tile(i)
+        return total + dot(chunk_vectors(i), tile, ((1,), (0,)))
+
+    narrow = lax.fori_loop(EARLY, 16, sketch_step, total)
 
     grams = [dot(n, n, ((1,), (1,)), HIGHEST) for n in (narrow[:, :LEAF], narrow[:, LEAF:])]
     root, scales = inverse_root(*grams)
@@ -339,7 +404,7 @@
         for n in range(2):
             at = unit * RANK + LINES * n
             b_ref[row + n] = rounded[at : at + LINES, :]
-    gather_b.start(0)
+    gather_b.start(gather_b.first(0))
 
     packed = rounded.astype(f32)
     sc_ref[...] = packed
@@ -367,21 +432,26 @@
 
     lax.fori_loop(0, PAIRS // GROUP, near_step, 0)
 
-    gather_b.wait(0)
-    gather_b.start(1)
-    gather_b.wait(1)
-    gather_b.start(2)
-    gather_b.start(3)
-    gather_b.side_start(0)
-    gather_b.wait(2)
-    gather_b.start(4)
-    gather_b.wait(3)
-    gather_b.side_start(1)
-    gather_b.side_start(2)
-    gather_b.wait(4)
-    gather_b.side_start(3)
-    for piece in range(4):
-        gather_b.side_wait(piece)
+    gather_b.second()
+    gather_b.third()
+
+    def near_planes(r, carry):
+        gather_b.pass_near(r)
+        return carry
+
+    def far_planes(r, carry):
+        gather_b.pass_far(r)
+        return carry
+
+    def siblings(r, carry):
+        gather_b.wait(gather_b.side_near(r))
+        gather_b.wait(gather_b.side_far(r))
+        return carry
+
+    lax.fori_loop(0, 4, near_planes, 0)
+    lax.fori_loop(0, 4, far_planes, 0)
+    gather_b.wait(gather_b.side_own())
+    lax.fori_loop(0, 4, siblings, 0)
 
     def far_step(g, carry):
         for pair in range(GROUP):
@@ -427,10 +497,12 @@
             jax.ShapeDtypeStruct((2, 128, 128), bf16),
             jax.ShapeDtypeStruct((PAIRS, RANK * RANK), f32),
         ),
-        in_specs=[vmem, vmem, vmem, smem, smem],
+        in_specs=[pl.BlockSpec(memory_space=pl.ANY), vmem, vmem, smem, smem],
         out_specs=(vmem, vmem),
         scratch_shapes=[
+            pltpu.VMEM((2, coords.shape[0], points // INPUTS), f32),
             pltpu.VMEM((points // UNIT, coords.shape[0], UNIT), f32),
+            pltpu.VMEM((EARLY, CHUNK, OWN), bf16),
             pltpu.VMEM((2 * CORE_ROWS // LINES, LINES, 128), bf16),
             pltpu.VMEM((2 * CORE_ROWS // LINES, LINES, 128), bf16),
             pltpu.VMEM((PAIRS, LEAF, LEAF), bf16),
@@ -441,14 +513,15 @@
             pltpu.VMEM((LEAF, 128), f32),
             pltpu.VMEM((2 * 128, 128), f32),
             pltpu.VMEM((GROUP * RANK // 2, 128), f32),
-            sems((3, 12)),
-            sems((3, 12)),
-            sems((3, 4)),
-            sems((3, 4)),
-            sems((3, 12)),
-            sems((3, 12)),
-            sems((3, 4)),
-            sems((3, 4)),
+            sems((2,)),
+            sems((3, 18)),
+            sems((3, 18)),
+            sems((3, 13)),
+            sems((3, 13)),
+            sems((3, 18)),
+            sems((3, 18)),
+            sems((3, 13)),
+            sems((3, 13)),
         ],
         compiler_params=pltpu.CompilerParams(
             collective_id=0, has_side_effects=True, vmem_limit_bytes=60 * 2**20

time: 97.8 us -> 96 us (0.982)
  Pallas kernels: 93.2 us -> 91.2 us
    pallas_call x1, Pallas kernels: 93.2 us -> 91.2 us  [per_device(): pl.pallas_call(kernel, out_shape=(jax.ShapeDtypeStruct((2, 128, 128), bf1...]
where the time goes in v3:
time: 96 us; the launch traced here: 95.7 us
  Pallas kernels  91.2 us (95%)
  local copies, waits for them, and re-layouts  3.81 us (4%)
    pallas_call x1, Pallas kernels, per_device(): pl.pallas_call(kernel, out_shape=(jax.ShapeDtypeStruct((2, 128, 128), bf1...  91.2 us
    unnamed x2, local copies, waits for them, and re-layouts  3.81 us

profile of v3, /device:TPU:1, one launch (start us, length us, event | category | flops | bytes accessed | tf_op | source)
XLA Modules:
  0.0 95.7 jit_solution(8965938414059287492)
XLA Ops:
  0.6 91.2 %shard_map.68 = (bf16[2,128,128]{2,1,0:T(8,128)(2,1)}, f32[64,4096]{1,0:T(8,128)}) custom-call(f32[16,65536]{1,0:T(8,128)} %coords.1, bf16[512,128]{1,0:T(8,128)(2,1)} %panel.1, f32[64,128]{1,0:T(8,128)} %bitcast.9, s32[1,64]{1,0:T(1,128)} %bitcast.11, s32[2,64]{1,0:T(2,128)} %bitcast.10), custom_call_target="tpu_custom_call" | custom-call | tf_op jit(solution)/shard_map/pallas_call | solution.py:494
  91.9 1.5 %copy.9 = bf16[1,2,128,128]{3,1,2,0:T(2,128)(2,1)} copy(bf16[1,2,128,128]{3,2,1,0:T(8,128)(2,1)} %bitcast.8) | data formatting | bytes 131072
  93.4 2.3 %copy.11 = f32[64,4096]{1,0:T(8,128)} copy(f32[64,4096]{1,0:T(8,128)} %get-tuple-element.9) | data formatting | bytes 2097152

commit v4 on v3

--- a/solution.py
+++ b/solution.py
@@ -42,6 +42,10 @@
     return jnp.where(k == 0, a, jnp.where(k == 1, b, c))
 
 
+def back(j):
+    return jnp.where(j == 0, 0, lax.rem(j, 3) + 1)
+
+
 def split3(v):
     hi = v.astype(bf16)
     rest = v - hi.astype(f32)
@@ -128,19 +132,17 @@
             result += [self.copy(part, stage, ref, s, 3 * stage + s - 1) for s in (1, 2, 3)]
         return result
 
-    def near_plane(self, r):
+    def near_plane(self, j):
         result = []
         for part in range(3):
             u = self.place.along(self.turn(part))
-            ref = self.ref(part, u[2], u[1] + r, 0, 4)
-            result += [
-                self.copy(part, 2, ref, s, 6 + 2 * r + way) for way, s in enumerate((1, SIDE - 1))
-            ]
+            for way, (r, s) in enumerate(((j, 1), (back(j), SIDE - 1))):
+                ref = self.ref(part, u[2], u[1] + r, 0, 4)
+                result.append(self.copy(part, 2, ref, s, 6 + 2 * j + way))
         return result
 
     def far_plane(self, r):
-        way = lax.div(r, 2)
-        step = 1 + 2 * way
+        step = 1 + 2 * lax.div(r, 2)
         result = []
         for part in range(3):
             u = self.place.along(self.turn(part))
@@ -165,13 +167,13 @@
             result.append(self.side(self.ref(part, u[2], 0, 0, 16), part, 0))
         return result
 
-    def side_near(self, r):
+    def side_near(self, j):
         result = []
         for part in range(3):
             u = self.place.along(self.turn(part))
-            for way, plane in enumerate((3, 1)):
+            for way, (r, plane) in enumerate(((j, 3), (back(j), 1))):
                 ref = self.ref(part, u[2] + plane, u[1] + r, 0, 4)
-                result.append(self.side(ref, part, 1 + 2 * r + way))
+                result.append(self.side(ref, part, 1 + 2 * j + way))
         return result
 
     def side_far(self, r):
@@ -200,10 +202,15 @@
             self.start(self.near_plane(r))
         self.start(self.side_own())
 
-    def pass_near(self, r):
-        self.wait(self.near_plane(r))
-        self.start(self.far_plane(r))
-        self.start(self.side_near(r))
+    def pass_near(self, j):
+        self.wait(self.near_plane(j))
+        for r, when in enumerate((0, 1, 1, 2)):
+
+            @pl.when(j == when)
+            def _(r=r):
+                self.start(self.far_plane(r))
+
+        self.start(self.side_near(j))
 
     def pass_far(self, r):
         self.wait(self.far_plane(r))
@@ -231,30 +238,32 @@
         lax.fori_loop(0, 4, step, 0)
 
 
-def inverse_root(gram0, gram1):
-    scales = [jnp.sqrt(jnp.sum(g * g) + EPSILON) for g in (gram0, gram1)]
-    zero = jnp.zeros((RANK, RANK), f32)
-    iterate = jnp.concatenate(
-        [
-            jnp.concatenate([gram0 / scales[0], zero], axis=1),
-            jnp.concatenate([zero, gram1 / scales[1]], axis=1),
-        ],
-        axis=0,
-    )
+def dot3(a, b):
+    ah, bh = a.astype(bf16), b.astype(bf16)
+    al, bl = (a - ah.astype(f32)).astype(bf16), (b - bh.astype(f32)).astype(bf16)
+    by = ((1,), (0,))
+    return dot(ah, bh, by) + (dot(ah, bl, by) + dot(al, bh, by))
+
+
+def inverse_root(stacked, left):
     shape = (2 * RANK, 2 * RANK)
-    ident = jnp.where(
-        lax.broadcasted_iota(jnp.int32, shape, 0) == lax.broadcasted_iota(jnp.int32, shape, 1),
-        1.0,
-        0.0,
-    )
+    row = lax.broadcasted_iota(jnp.int32, shape, 0)
+    col = lax.broadcasted_iota(jnp.int32, shape, 1)
+    gram = jnp.where((row < RANK) == (col < RANK), dot(stacked, stacked, ((1,), (1,)), HIGHEST), 0.0)
+    sums = jnp.sum(gram * gram, axis=0, keepdims=True)
+    zero = jnp.zeros_like(sums)
+    sums = [jnp.sum(v, axis=1, keepdims=True) for v in (jnp.where(left, sums, zero), jnp.where(left, zero, sums))]
+    scale = jnp.sqrt(jnp.where(left, sums[0], sums[1]) + EPSILON)
+    iterate = gram / scale
+    ident = jnp.where(row == col, 1.0, 0.0)
     root = ident
     for sweep in range(NSWEEPS):
-        product = iterate if sweep == 0 else dot(root, iterate, ((1,), (0,)), HIGHEST)
+        product = iterate if sweep == 0 else dot3(root, iterate)
         factor = 1.5 * ident - 0.5 * product
         if sweep < NSWEEPS - 1:
-            iterate = dot(iterate, factor, ((1,), (0,)), HIGHEST)
-        root = factor if sweep == 0 else dot(factor, root, ((1,), (0,)), HIGHEST)
-    return root, scales
+            iterate = dot3(iterate, factor)
+        root = factor if sweep == 0 else dot3(factor, root)
+    return root, scale
 
 
 def kernel(
@@ -270,11 +279,11 @@
 
     def load(j):
         return pltpu.make_async_copy(
-            coords.at[:, j * width : (j + 1) * width], in_ref.at[j % 2], in_sem.at[j % 2]
+            coords.at[:, j * width : (j + 1) * width], in_ref.at[j % 4], in_sem.at[j % 4]
         )
 
-    load(0).start()
-    load(1).start()
+    for j in range(4):
+        load(j).start()
     barrier = pltpu.get_barrier_semaphore()
     peers = [place.neighbour(axis, step) for axis in range(3) for step in (1, 2, 3)]
     peers.append(place.sibling())
@@ -291,9 +300,9 @@
     for j in range(INPUTS):
         load(j).wait()
         for unit in range(width // UNIT):
-            x_ref[j * width // UNIT + unit] = in_ref[j % 2, :, unit * UNIT : (unit + 1) * UNIT]
-        if j + 2 < INPUTS:
-            load(j + 2).start()
+            x_ref[j * width // UNIT + unit] = in_ref[j % 4, :, unit * UNIT : (unit + 1) * UNIT]
+        if j + 4 < INPUTS:
+            load(j + 4).start()
     own = [x_ref[place.index * UNITS + unit] for unit in range(UNITS)]
     own_features = features(jnp.concatenate(own, axis=1), False)
     g_ref[...] = own_features
@@ -323,7 +332,7 @@
         other = jnp.where(in_own, lax.div(i, 2), lax.rem(i, 2))
         core = lax.rem(place.core + other, 2)
         r = jnp.where(in_far, lax.div(i + 4, 2) - 8, jnp.where(in_own, 2 * lax.rem(i, 2), lax.div(i, 2) - 2))
-        groups = (r, r + jnp.where(in_far, 2, jnp.where(in_own, 1, 0)))
+        groups = (r, jnp.where(in_far, r + 2, jnp.where(in_own, r + 1, back(r))))
         planes = [jnp.where(in_far, 2, jnp.where(in_own, 0, p)) for p in (3, 1)]
         units = []
         for half in range(2):
@@ -394,11 +403,10 @@
 
     narrow = lax.fori_loop(EARLY, 16, sketch_step, total)
 
-    grams = [dot(n, n, ((1,), (1,)), HIGHEST) for n in (narrow[:, :LEAF], narrow[:, LEAF:])]
-    root, scales = inverse_root(*grams)
     stacked = jnp.concatenate([narrow[:, :LEAF], narrow[:, LEAF:]], axis=0)
     left = lax.broadcasted_iota(jnp.int32, (1, 2 * RANK), 1) < RANK
-    scale = jnp.sqrt(jnp.where(left, scales[0], scales[1]))
+    root, scale = inverse_root(stacked, left)
+    scale = jnp.sqrt(scale)
     rounded = (dot(stacked, root, ((0,), (0,)), HIGHEST) / scale).astype(bf16)
     for unit, row in enumerate(gather_b.own_rows()):
         for n in range(2):
@@ -500,7 +508,7 @@
         in_specs=[pl.BlockSpec(memory_space=pl.ANY), vmem, vmem, smem, smem],
         out_specs=(vmem, vmem),
         scratch_shapes=[
-            pltpu.VMEM((2, coords.shape[0], points // INPUTS), f32),
+            pltpu.VMEM((4, coords.shape[0], points // INPUTS), f32),
             pltpu.VMEM((points // UNIT, coords.shape[0], UNIT), f32),
             pltpu.VMEM((EARLY, CHUNK, OWN), bf16),
             pltpu.VMEM((2 * CORE_ROWS // LINES, LINES, 128), bf16),
@@ -513,7 +521,7 @@
             pltpu.VMEM((LEAF, 128), f32),
             pltpu.VMEM((2 * 128, 128), f32),
             pltpu.VMEM((GROUP * RANK // 2, 128), f32),
-            sems((2,)),
+            sems((4,)),
             sems((3, 18)),
             sems((3, 18)),
             sems((3, 13)),

time: 96 us -> 93.8 us (0.977)
  Pallas kernels: 91.2 us -> 89.1 us
    pallas_call x1, Pallas kernels: 91.2 us -> 89.1 us  [per_device(): pl.pallas_call(kernel, out_shape=(jax.ShapeDtypeStruct((2, 128, 128), bf1...]
where the time goes in v4:
time: 93.8 us; the launch traced here: 93.6 us
  Pallas kernels  89.1 us (95%)
  local copies, waits for them, and re-layouts  3.81 us (4%)
    pallas_call x1, Pallas kernels, per_device(): pl.pallas_call(kernel, out_shape=(jax.ShapeDtypeStruct((2, 128, 128), bf1...  89.1 us
    unnamed x2, local copies, waits for them, and re-layouts  3.81 us

profile of v4, /device:TPU:1, one launch (start us, length us, event | category | flops | bytes accessed | tf_op | source)
XLA Modules:
  0.0 93.6 jit_solution(15509911751771397823)
XLA Ops:
  0.6 89.1 %shard_map.68 = (bf16[2,128,128]{2,1,0:T(8,128)(2,1)}, f32[64,4096]{1,0:T(8,128)}) custom-call(f32[16,65536]{1,0:T(8,128)} %coords.1, bf16[512,128]{1,0:T(8,128)(2,1)} %panel.1, f32[64,128]{1,0:T(8,128)} %bitcast.9, s32[1,64]{1,0:T(1,128)} %bitcast.11, s32[2,64]{1,0:T(2,128)} %bitcast.10), custom_call_target="tpu_custom_call" | custom-call | tf_op jit(solution)/shard_map/pallas_call | solution.py:502
  89.8 1.5 %copy.9 = bf16[1,2,128,128]{3,1,2,0:T(2,128)(2,1)} copy(bf16[1,2,128,128]{3,2,1,0:T(8,128)(2,1)} %bitcast.8) | data formatting | bytes 131072
  91.3 2.3 %copy.11 = f32[64,4096]{1,0:T(8,128)} copy(f32[64,4096]{1,0:T(8,128)} %get-tuple-element.9) | data formatting | bytes 2097152

commit v5 on v4

--- a/solution.py
+++ b/solution.py
@@ -24,8 +24,8 @@
 LINES = 32
 SIDE = 4
 CHUNK = 4096
-EARLY = 3
-INPUTS = 8
+EARLY = 6
+INPUTS = 16
 PART_UNITS = (2, 1, 1)
 PART_ROWS = tuple(RANK * u for u in PART_UNITS)
 PART_BASE = (0, 128 * SIDE**3, 192 * SIDE**3)
@@ -268,7 +268,7 @@
 
 def kernel(
     coords, panel, mixing, owners, picks, bases_out, coup_out,
-    in_ref, x_ref, pre_ref, q_ref, b_ref, k_ref, g_ref, gt_ref, l_ref, bs_ref, sc_ref, sct_ref, st_ref,
+    in_ref, x_ref, pre_ref, q_ref, b_ref, g_ref, gt_ref, l_ref, bs_ref, sc_ref, sct_ref, st_ref,
     in_sem, q_send, q_recv, q_sib_send, q_sib_recv, b_send, b_recv, b_sib_send, b_sib_recv,
 ):
     place = Place()
@@ -294,9 +294,6 @@
     for unit, row in enumerate(gather_q.own_rows()):
         for n in range(2):
             q_ref[row + n] = vectors[LINES * n : LINES * (n + 1), unit * UNIT : (unit + 1) * UNIT]
-    pl.semaphore_wait(barrier, len(peers))
-
-    gather_q.start(gather_q.first(0))
     for j in range(INPUTS):
         load(j).wait()
         for unit in range(width // UNIT):
@@ -309,24 +306,9 @@
     for leaf in range(2):
         gt_ref[leaf] = own_features[:, leaf * LEAF : (leaf + 1) * LEAF].T
 
-    def pair_step(g, carry):
-        @pl.when(g == 6)
-        def _():
-            gather_q.second()
-
-        far = []
-        for n in range(GROUP):
-            entry = (owners[0, g * GROUP + n] * 2 + picks[1, g * GROUP + n]) * 2
-            far += [x_ref[entry], x_ref[entry + 1]]
-        far = features(jnp.concatenate(far, axis=1), True)
-        for n in range(GROUP):
-            near_rows = gt_ref[picks[0, g * GROUP + n]]
-            exponent = dot(near_rows, far[:, n * LEAF : (n + 1) * LEAF], ((1,), (0,)))
-            k_ref[g * GROUP + n] = jnp.exp2(exponent).astype(bf16)
-        return carry
-
-    lax.fori_loop(0, PAIRS // GROUP, pair_step, 0)
-
+    pl.semaphore_wait(barrier, len(peers))
+
+    gather_q.start(gather_q.first(0))
     def chunk(i):
         in_own, in_far = i < 4, i >= 12
         other = jnp.where(in_own, lax.div(i, 2), lax.rem(i, 2))
@@ -359,26 +341,22 @@
         return jnp.concatenate(vectors, axis=1)
 
     def early_tile(i, carry):
+        @pl.when(i == 4)
+        def _():
+            gather_q.second()
+
         pre_ref[i] = chunk_tile(i)
         return carry
 
     lax.fori_loop(0, EARLY, early_tile, 0)
     gather_q.third()
 
-    def await_side(i):
+    def arrive(i):
+        even = lax.rem(i, 2) == 0
+
         @pl.when(i == 2)
         def _():
             gather_q.wait(gather_q.side_own())
-
-    def early_step(i, total):
-        await_side(i)
-        return total + dot(chunk_vectors(i), pre_ref[i], ((1,), (0,)))
-
-    total = lax.fori_loop(0, EARLY, early_step, jnp.zeros((RANK, OWN), f32))
-
-    def sketch_step(i, total):
-        await_side(i)
-        even = lax.rem(i, 2) == 0
 
         @pl.when((i >= 4) & (i < 12) & even)
         def _():
@@ -398,6 +376,14 @@
             gather_q.wait(gather_q.side_far(lax.div(i, 2) - 6))
             gather_q.wait(gather_q.side_far(lax.div(i, 2) - 4))
 
+    def early_step(i, total):
+        arrive(i)
+        return total + dot(chunk_vectors(i), pre_ref[i], ((1,), (0,)))
+
+    total = lax.fori_loop(0, EARLY, early_step, jnp.zeros((RANK, OWN), f32))
+
+    def sketch_step(i, total):
+        arrive(i)
         tile = chunk_tile(i)
         return total + dot(chunk_vectors(i), tile, ((1,), (0,)))
 
@@ -433,14 +419,27 @@
                 ].astype(bf16)
 
     def near_step(g, carry):
+        @pl.when(g == 5)
+        def _():
+            gather_b.second()
+
+        far = []
         for n in range(GROUP):
+            entry = (owners[0, g * GROUP + n] * 2 + picks[1, g * GROUP + n]) * 2
+            far += [x_ref[entry], x_ref[entry + 1]]
+        far = features(jnp.concatenate(far, axis=1), True)
+        tiles = []
+        for n in range(GROUP):
+            near_rows = gt_ref[picks[0, g * GROUP + n]]
+            exponent = dot(near_rows, far[:, n * LEAF : (n + 1) * LEAF], ((1,), (0,)))
+            tiles.append(jnp.exp2(exponent).astype(bf16))
+        for n, tile in enumerate(tiles):
             k = g * GROUP + n
-            l_ref[k] = dot(bs_ref[picks[0, k]], k_ref[k], ((1,), (0,))).astype(bf16)
+            l_ref[k] = dot(bs_ref[picks[0, k]], tile, ((1,), (0,))).astype(bf16)
         return carry
 
     lax.fori_loop(0, PAIRS // GROUP, near_step, 0)
 
-    gather_b.second()
     gather_b.third()
 
     def near_planes(r, carry):
@@ -513,7 +512,6 @@
             pltpu.VMEM((EARLY, CHUNK, OWN), bf16),
             pltpu.VMEM((2 * CORE_ROWS // LINES, LINES, 128), bf16),
             pltpu.VMEM((2 * CORE_ROWS // LINES, LINES, 128), bf16),
-            pltpu.VMEM((PAIRS, LEAF, LEAF), bf16),
             pltpu.VMEM((128, OWN), bf16),
             pltpu.VMEM((2, LEAF, 128), bf16),
             pltpu.VMEM((PAIRS, RANK, LEAF), bf16),

time: 93.8 us -> 93.7 us (level)
  no operation moved by 1% of the time
where the time goes in v5:
time: 93.7 us; the launch traced here: 93.4 us
  Pallas kernels  89 us (95%)
  local copies, waits for them, and re-layouts  3.81 us (4%)
    pallas_call x1, Pallas kernels, per_device(): pl.pallas_call(kernel, out_shape=(jax.ShapeDtypeStruct((2, 128, 128), bf1...  89 us
    unnamed x2, local copies, waits for them, and re-layouts  3.81 us

profile of v5, /device:TPU:1, one launch (start us, length us, event | category | flops | bytes accessed | tf_op | source)
XLA Modules:
  0.0 93.4 jit_solution(10921879047383712326)
XLA Ops:
  0.6 89.0 %shard_map.68 = (bf16[2,128,128]{2,1,0:T(8,128)(2,1)}, f32[64,4096]{1,0:T(8,128)}) custom-call(f32[16,65536]{1,0:T(8,128)} %coords.1, bf16[512,128]{1,0:T(8,128)(2,1)} %panel.1, f32[64,128]{1,0:T(8,128)} %bitcast.9, s32[1,64]{1,0:T(1,128)} %bitcast.11, s32[2,64]{1,0:T(2,128)} %bitcast.10), custom_call_target="tpu_custom_call" | custom-call | tf_op jit(solution)/shard_map/pallas_call | solution.py:501
  89.6 1.5 %copy.9 = bf16[1,2,128,128]{3,1,2,0:T(2,128)(2,1)} copy(bf16[1,2,128,128]{3,2,1,0:T(8,128)(2,1)} %bitcast.8) | data formatting | bytes 131072
  91.2 2.3 %copy.11 = f32[64,4096]{1,0:T(8,128)} copy(f32[64,4096]{1,0:T(8,128)} %get-tuple-element.9) | data formatting | bytes 2097152

commit v6 on v5

--- a/solution.py
+++ b/solution.py
@@ -406,8 +406,10 @@
     for side in range(2):
         sct_ref[128 * side : 128 * (side + 1), :] = flipped[:, 128 * side : 128 * (side + 1)]
     even, odd = sc_ref[pl.ds(0, 128, stride=2), :], sc_ref[pl.ds(1, 128, stride=2), :]
-    bases_out[0] = jnp.where(left, even, pltpu.roll(odd, RANK, 1)).astype(bf16)
-    bases_out[1] = jnp.where(left, pltpu.roll(even, RANK, 1), odd).astype(bf16)
+    sc_ref[:128, :] = jnp.where(left, even, pltpu.roll(odd, RANK, 1))
+    sc_ref[128:, :] = jnp.where(left, pltpu.roll(even, RANK, 1), odd)
+    for i in range(128):
+        bases_out[:, 128 * i : 128 * (i + 1)] = sc_ref[pl.ds(i, 2, stride=128), :].astype(bf16)
     half = RANK // 2
     for leaf in range(2):
         for odd_one in range(2):
@@ -501,8 +503,8 @@
     bases, couplings = pl.pallas_call(
         kernel,
         out_shape=(
-            jax.ShapeDtypeStruct((2, 128, 128), bf16),
-            jax.ShapeDtypeStruct((PAIRS, RANK * RANK), f32),
+            pltpu.VMEM((2, LEAF * RANK), bf16),
+            pltpu.VMEM((PAIRS, RANK * RANK), f32),
         ),
         in_specs=[pl.BlockSpec(memory_space=pl.ANY), vmem, vmem, smem, smem],
         out_specs=(vmem, vmem),
@@ -533,7 +535,7 @@
             collective_id=0, has_side_effects=True, vmem_limit_bytes=60 * 2**20
         ),
     )(coords, panel, mixing.T, owners.T, leaf_picks.T)
-    return bases.reshape(2, LEAF * RANK), couplings
+    return bases, couplings
 
 
 def solution(mesh):

time: 93.7 us -> 90.4 us (0.965)
  local copies, waits for them, and re-layouts: 3.81 us -> 1.6 us
  Pallas kernels: 89 us -> 88 us
    unnamed x2, local copies, waits for them, and re-layouts: 3.81 us -> 1.6 us
    pallas_call x1, Pallas kernels: 89 us -> 88 us  [per_device(): pl.pallas_call(kernel, out_shape=(pltpu.VMEM((2, LEAF * RANK), bf16), plt...]
where the time goes in v6:
time: 90.4 us; the launch traced here: 90.2 us
  Pallas kernels  88 us (97%)
  local copies, waits for them, and re-layouts  1.6 us (2%)
    pallas_call x1, Pallas kernels, per_device(): pl.pallas_call(kernel, out_shape=(pltpu.VMEM((2, LEAF * RANK), bf16), plt...  88 us

profile of v6, /device:TPU:1, one launch (start us, length us, event | category | flops | bytes accessed | tf_op | source)
XLA Modules:
  0.0 90.2 jit_solution(8747057628347495148)
XLA Ops:
  0.6 88.0 %shard_map.68 = (bf16[2,16384]{1,0:T(2,128)(2,1)S(1)}, f32[64,4096]{1,0:T(8,128)S(1)}) custom-call(f32[16,65536]{1,0:T(8,128)} %coords.1, bf16[512,128]{1,0:T(8,128)(2,1)} %panel.1, f32[64,128]{1,0:T(8,128)} %bitcast.3, s32[1,64]{1,0:T(1,128)} %bitcast.5, s32[2,64]{1,0:T(2,128)} %bitcast.4), custom_call_target="tpu_custom_call" | custom-call | tf_op jit(solution)/shard_map/pallas_call | solution.py:503
  88.6 0.6 copy.9
  89.2 1.0 %copy.10 = f32[64,4096]{1,0:T(8,128)} copy(f32[64,4096]{1,0:T(8,128)S(1)} %get-tuple-element.3) | data formatting | bytes 2097152

commit v7 on v6

--- a/solution.py
+++ b/solution.py
@@ -24,7 +24,7 @@
 LINES = 32
 SIDE = 4
 CHUNK = 4096
-EARLY = 6
+EARLY = 7
 INPUTS = 16
 PART_UNITS = (2, 1, 1)
 PART_ROWS = tuple(RANK * u for u in PART_UNITS)
@@ -268,7 +268,7 @@
 
 def kernel(
     coords, panel, mixing, owners, picks, bases_out, coup_out,
-    in_ref, x_ref, pre_ref, q_ref, b_ref, g_ref, gt_ref, l_ref, bs_ref, sc_ref, sct_ref, st_ref,
+    in_ref, x_ref, pre_ref, q_ref, b_ref, g_ref, gt_ref, bs_ref, sc_ref, sct_ref, st_ref,
     in_sem, q_send, q_recv, q_sib_send, q_sib_recv, b_send, b_recv, b_sib_send, b_sib_recv,
 ):
     place = Place()
@@ -437,7 +437,8 @@
             tiles.append(jnp.exp2(exponent).astype(bf16))
         for n, tile in enumerate(tiles):
             k = g * GROUP + n
-            l_ref[k] = dot(bs_ref[picks[0, k]], tile, ((1,), (0,))).astype(bf16)
+            rows = pl.ds(pl.multiple_of(k * RANK, RANK), RANK)
+            pre_ref[0, rows, :LEAF] = dot(bs_ref[picks[0, k]], tile, ((1,), (0,))).astype(bf16)
         return carry
 
     lax.fori_loop(0, PAIRS // GROUP, near_step, 0)
@@ -463,6 +464,7 @@
     lax.fori_loop(0, 4, siblings, 0)
 
     def far_step(g, carry):
+        products = []
         for pair in range(GROUP):
             k = g * GROUP + pair
             line, col = lax.div(owners[0, k], 16), lax.rem(owners[0, k], 16)
@@ -475,11 +477,11 @@
                 row = core * (CORE_ROWS // LINES) + PART_BASE[part] // LINES + slot * (PART_ROWS[part] // LINES)
                 for n in range(PART_ROWS[part] // LINES):
                     blocks.append(b_ref[row + n])
-            both = dot(
-                l_ref[k],
-                jnp.concatenate(blocks, axis=0),
-                ((1,), (0,)),
-            )
+            rows = pl.ds(pl.multiple_of(k * RANK, RANK), RANK)
+            near = pre_ref[0, rows, :LEAF]
+            products.append(dot(near, jnp.concatenate(blocks, axis=0), ((1,), (0,))))
+        for pair, both in enumerate(products):
+            k = g * GROUP + pair
             even, odd = both[:half, :], both[half:, :]
             first = jnp.where(left, even, pltpu.roll(odd, RANK, 1))
             second = jnp.where(left, pltpu.roll(even, RANK, 1), odd)
@@ -516,7 +518,6 @@
             pltpu.VMEM((2 * CORE_ROWS // LINES, LINES, 128), bf16),
             pltpu.VMEM((128, OWN), bf16),
             pltpu.VMEM((2, LEAF, 128), bf16),
-            pltpu.VMEM((PAIRS, RANK, LEAF), bf16),
             pltpu.VMEM((2, RANK, LEAF), bf16),
             pltpu.VMEM((LEAF, 128), f32),
             pltpu.VMEM((2 * 128, 128), f32),

time: 90.4 us -> 90.8 us (level)
  no operation moved by 1% of the time
where the time goes in v7:
time: 90.8 us; the launch traced here: 90.6 us
  Pallas kernels  88.4 us (97%)
  local copies, waits for them, and re-layouts  1.6 us (2%)
    pallas_call x1, Pallas kernels, per_device(): pl.pallas_call(kernel, out_shape=(pltpu.VMEM((2, LEAF * RANK), bf16), plt...  88.4 us

profile of v7, /device:TPU:1, one launch (start us, length us, event | category | flops | bytes accessed | tf_op | source)
XLA Modules:
  0.0 90.6 jit_solution(2209029391405073919)
XLA Ops:
  0.6 88.4 %shard_map.68 = (bf16[2,16384]{1,0:T(2,128)(2,1)S(1)}, f32[64,4096]{1,0:T(8,128)S(1)}) custom-call(f32[16,65536]{1,0:T(8,128)} %coords.1, bf16[512,128]{1,0:T(8,128)(2,1)} %panel.1, f32[64,128]{1,0:T(8,128)} %bitcast.3, s32[1,64]{1,0:T(1,128)} %bitcast.5, s32[2,64]{1,0:T(2,128)} %bitcast.4), custom_call_target="tpu_custom_call" | custom-call | tf_op jit(solution)/shard_map/pallas_call | solution.py:505
  89.0 0.6 copy.9
  89.6 1.0 %copy.10 = f32[64,4096]{1,0:T(8,128)} copy(f32[64,4096]{1,0:T(8,128)S(1)} %get-tuple-element.3) | data formatting | bytes 2097152

commit v8 on v6

--- a/solution.py
+++ b/solution.py
@@ -341,7 +341,7 @@
         return jnp.concatenate(vectors, axis=1)
 
     def early_tile(i, carry):
-        @pl.when(i == 4)
+        @pl.when(i == 3)
         def _():
             gather_q.second()
 

time: 90.4 us -> 88.6 us (0.980)
  Pallas kernels: 88 us -> 86.2 us
    pallas_call x1, Pallas kernels: 88 us -> 86.2 us  [per_device(): pl.pallas_call(kernel, out_shape=(pltpu.VMEM((2, LEAF * RANK), bf16), plt...]
where the time goes in v8:
time: 88.6 us; the launch traced here: 88.4 us
  Pallas kernels  86.2 us (97%)
  local copies, waits for them, and re-layouts  1.6 us (2%)
    pallas_call x1, Pallas kernels, per_device(): pl.pallas_call(kernel, out_shape=(pltpu.VMEM((2, LEAF * RANK), bf16), plt...  86.2 us

profile of v8, /device:TPU:1, one launch (start us, length us, event | category | flops | bytes accessed | tf_op | source)
XLA Modules:
  0.0 88.4 jit_solution(12214459536036277534)
XLA Ops:
  0.6 86.2 %shard_map.68 = (bf16[2,16384]{1,0:T(2,128)(2,1)S(1)}, f32[64,4096]{1,0:T(8,128)S(1)}) custom-call(f32[16,65536]{1,0:T(8,128)} %coords.1, bf16[512,128]{1,0:T(8,128)(2,1)} %panel.1, f32[64,128]{1,0:T(8,128)} %bitcast.3, s32[1,64]{1,0:T(1,128)} %bitcast.5, s32[2,64]{1,0:T(2,128)} %bitcast.4), custom_call_target="tpu_custom_call" | custom-call | tf_op jit(solution)/shard_map/pallas_call | solution.py:503
  86.8 0.6 copy.9
  87.5 1.0 %copy.10 = f32[64,4096]{1,0:T(8,128)} copy(f32[64,4096]{1,0:T(8,128)S(1)} %get-tuple-element.3) | data formatting | bytes 2097152
